TPU v7x, 32 devices: a whole 2x2x4 slice. The times are simulated.
32 devices in a mesh: dom: 8 (over z, x), cls: 4 (over y, core).
Axes of the slice: x: 2, y: 2, z: 4, core: 2. Of those that a mesh axis runs over, the one named last changes fastest.
Arguments:
- images: bfloat16 [4096, 4096], P(('dom', 'cls')), may hold values from -96 to 96
- destinations: int32 [4096, 1], P(('dom', 'cls')), may hold values from 0 to 7; in each aligned block of 128 rows (0 to 127, 128 to 255, ...) at most 32 rows name the same one
- group_ids: int32 [4096], P(('dom', 'cls')), may hold values from 0 to 15
- offsets: int32 [3, 2], replicated, may hold values from -4 to 4
- inv_noise: float32 [2048], replicated, may hold values from 0.02 to 0.2
- ctf_table: float32 [16, 2048], replicated, may hold values from -1 to 1
- references: bfloat16 [288, 4096], P('cls', 'dom'), may hold values from -16 to 16
Outputs:
- posteriors: float32 [8192, 288], P('dom', 'cls')
- log_norms: float32 [8192], P('dom')
Inputs may be any that keep to these rules, and one draw needn't show every extreme that they name: `destinations`: in the rows of one device no destination is named more than 32 times.
All inputs are finite; a program needn't handle non-finite values.
Results may differ from a plain program's by a relative error of at most 0.00061.
Values may be sent and summed in bfloat16 or wider, within the bound.
A program may use at most 64 MiB of HBM per device.

v0:
```python
import math

import jax
import jax.numpy as jnp
from jax import lax
from jax.sharding import PartitionSpec as P

SIDE = 64
F = 2048
NT = 3
G = 16


def phase_tables(offsets):
    freq_index = jnp.arange(F, dtype=jnp.int32)
    half_side = SIDE // 2
    row_freq = freq_index // half_side
    col_freq = freq_index % half_side
    row_freq = jnp.where(row_freq >= half_side, row_freq - SIDE, row_freq)
    turns = jnp.mod(offsets[:, 0:1] * row_freq[None, :] + offsets[:, 1:2] * col_freq[None, :], SIDE)
    angles = turns.astype(jnp.float32) * (2.0 * math.pi / SIDE)
    return (jnp.cos(angles), jnp.sin(angles))


def shifted_rows(slot_images, slot_groups, offsets, inv_noise, ctf_table):
    cosines, sines = phase_tables(offsets)
    group_hot = (slot_groups[:, None] == jnp.arange(G, dtype=jnp.int32)[None, :]).astype(
        jnp.float32
    )
    ctf_rows = jnp.dot(
        group_hot, ctf_table, precision=lax.Precision.HIGHEST, preferred_element_type=jnp.float32
    )
    weight = inv_noise[None, :] * ctf_rows
    real_part = slot_images[:, :F].astype(jnp.float32)
    imag_part = slot_images[:, F:].astype(jnp.float32)
    pieces = []
    for shift_index in range(NT):
        cosine = cosines[shift_index][None, :]
        sine = sines[shift_index][None, :]
        both = jnp.concatenate(
            [
                weight * (real_part * cosine - imag_part * sine),
                weight * (real_part * sine + imag_part * cosine),
            ],
            axis=1,
        )
        pieces.append(both.astype(jnp.bfloat16))
    return (jnp.concatenate(pieces, axis=0), group_hot)


def block_scores(cross_sum, norm_sum, group_hot, slot_count):
    selected = jnp.dot(
        group_hot, norm_sum, precision=lax.Precision.HIGHEST, preferred_element_type=jnp.float32
    )
    return cross_sum.reshape(NT, slot_count, -1) - 0.5 * selected[None, :, :]


def slot_posteriors(scores, slot_groups):
    row_peak = jnp.max(scores, axis=(0, 2))
    row_total = jnp.sum(jnp.exp(scores - row_peak[None, :, None]), axis=(0, 2))
    log_norm = row_peak + jnp.log(row_total)
    posterior = jnp.sum(jnp.exp(scores - log_norm[None, :, None]), axis=0)
    filled = slot_groups >= 0
    posterior = jnp.where(filled[:, None], posterior, 0.0)
    log_norm = jnp.where(filled, log_norm, 0.0)
    return (posterior, log_norm)


def shards(images, destinations, group_ids, offsets, inv_noise, ctf_table, references):
    dom_size = lax.axis_size("dom")
    local_count = images.shape[0]
    capacity = 2 * local_count // dom_size
    slot_count = dom_size * capacity
    class_rows = lax.all_gather(references, "cls", axis=0, tiled=True)
    every_ref = lax.all_gather(class_rows, "dom", axis=1, tiled=True)
    target = destinations[:, 0]
    target_hot = (target[:, None] == jnp.arange(dom_size, dtype=jnp.int32)[None, :]).astype(
        jnp.float32
    )
    local_index = jnp.arange(local_count, dtype=jnp.int32)
    lower = (local_index[:, None] > local_index[None, :]).astype(jnp.float32)
    earlier = jnp.dot(
        lower, target_hot, precision=lax.Precision.HIGHEST, preferred_element_type=jnp.float32
    )
    position_rank = jnp.sum(earlier * target_hot, axis=1).astype(jnp.int32)
    slot_of = target * capacity + position_rank
    chosen = jnp.arange(slot_count, dtype=jnp.int32)[:, None] == slot_of[None, :]
    send_images = jnp.dot(
        chosen.astype(jnp.bfloat16), images, preferred_element_type=jnp.float32
    ).astype(jnp.bfloat16)
    send_groups = jnp.sum(jnp.where(chosen, group_ids[None, :] + 1, 0), axis=1) - 1
    slot_images, slot_groups = (
        lax.all_to_all(send_images, "dom", split_axis=0, concat_axis=0, tiled=True),
        lax.all_to_all(send_groups, "dom", split_axis=0, concat_axis=0, tiled=True),
    )
    noise_ctf = inv_noise[None, :] * ctf_table * ctf_table
    noise_terms = jnp.concatenate([noise_ctf, noise_ctf], axis=1)
    shifted, group_hot = shifted_rows(slot_images, slot_groups, offsets, inv_noise, ctf_table)
    contract = (((1,), (1,)), ((), ()))
    cross_sum = lax.dot_general(shifted, every_ref, contract, preferred_element_type=jnp.float32)
    ref_float = every_ref.astype(jnp.float32)
    norm_sum = lax.dot_general(
        noise_terms,
        ref_float * ref_float,
        contract,
        precision=lax.Precision.HIGHEST,
        preferred_element_type=jnp.float32,
    )
    scores = block_scores(cross_sum, norm_sum, group_hot, slot_count)
    posterior, log_norm = slot_posteriors(scores, slot_groups)
    posteriors = lax.all_to_all(posterior, "cls", split_axis=1, concat_axis=0, tiled=True)
    log_norms = lax.all_gather(log_norm, "cls", axis=0, tiled=True)
    return (posteriors, log_norms)


def solution(mesh):
    return jax.shard_map(
        shards,
        mesh=mesh,
        in_specs=(
            P(("dom", "cls"), None),
            P(("dom", "cls"), None),
            P(("dom", "cls")),
            P(),
            P(),
            P(),
            P("cls", "dom"),
        ),
        out_specs=(P("dom", "cls"), P("dom")),
        check_vma=False,
    )
```

profile of v0, /device:TPU:0, one launch (start us, length us, event | category | flops | bytes accessed | tf_op | source)
XLA Modules:
  0.0 155.8 jit_solution(8169670739551059540)
XLA Ops:
  7.2 0.0 copy-start
  7.2 0.9 fusion.33
  8.1 0.7 convert_add_fusion
  8.8 0.1 select_reduce_fusion
  8.9 0.7 sub.61
  9.6 7.3 %all-to-all-start = ((s32[8,32,1]{1,2,0:T(1,128)}), s32[8,32,1]{1,2,0:T(1,128)S(1)}, u32[]{:S(2)}, u32[]{:S(2)}) async-start(s32[8,32,1]{1,2,0:T(1,128)} %bitcast.1), calls=%async_computation | async-start | bytes 8192 | tf_op jit(solution)/shard_map/all_to_all | solution.py:94
  16.8 0.0 copy-done
  16.8 2.0 %convolution_convert_fusion = bf16[256,4096]{1,0:T(8,128)(2,1)} fusion(bf16[128,4096]{1,0:T(8,128)(2,1)S(1)} %copy-done, s32[128]{0:T(128)S(1)} %get-tuple-element.28), kind=kOutput, calls=%fused_computation.12 | convolution fusion | flops 269516800 | bytes 3146240 | tf_op jit(solution)/shard_map/dot_general | solution.py:88
  18.9 4.4 %all-to-all-done = s32[8,32,1]{1,2,0:T(1,128)S(1)} async-done(((s32[8,32,1]{1,2,0:T(1,128)}), s32[8,32,1]{1,2,0:T(1,128)S(1)}, u32[]{:S(2)}, u32[]{:S(2)}) %all-to-all-start) | async-done | bytes 1056 | tf_op jit(solution)/shard_map/all_to_all | solution.py:94
  23.2 0.0 copy-start.2
  23.2 0.0 copy-start.4
  23.2 0.0 copy-start.1
  23.2 0.0 copy-start.3
  23.2 3.7 %all-to-all-start.1 = ((bf16[8,32,4096]{2,1,0:T(8,128)(2,1)}), bf16[8,32,4096]{2,1,0:T(8,128)(2,1)S(1)}, u32[]{:S(2)}, u32[]{:S(2)}) async-start(bf16[8,32,4096]{2,1,0:T(8,128)(2,1)} %bitcast.2), calls=%async_computation.1 | async-start | bytes 4194304 | tf_op jit(solution)/shard_map/all_to_all | solution.py:93
  27.0 0.0 all-gather.3.cloned.1.call-start
  27.0 0.0 copy-done.2
  27.0 6.4 %all_gather.9 = bf16[288,512]{1,0:T(8,128)(2,1)} all-gather(bf16[72,512]{1,0:T(8,128)(2,1)S(1)} %copy-done.2), channel_id=1, replica_groups=mesh['dom'=8,'cls'=4] {'cls'}, dimensions={0}, use_global_device_ids=true | all-gather | bytes 368640 | tf_op jit(solution)/shard_map/all_gather | solution.py:74
  33.4 0.0 all-gather.3.cloned.1.call-update
  33.5 0.0 copy-done.4
  33.5 0.3 fusion.48
  33.9 0.0 copy-done.1
  33.9 0.0 copy-done.3
  34.0 0.5 broadcast.124
  34.5 0.7 reduce.7
  35.1 0.1 all_to_all.27
  35.2 48.3 %all-to-all-done.1 = bf16[8,32,4096]{2,1,0:T(8,128)(2,1)S(1)} async-done(((bf16[8,32,4096]{2,1,0:T(8,128)(2,1)}), bf16[8,32,4096]{2,1,0:T(8,128)(2,1)S(1)}, u32[]{:S(2)}, u32[]{:S(2)}) %all-to-all-start.1) | async-done | bytes 2097184 | tf_op jit(solution)/shard_map/all_to_all | solution.py:93
  83.6 4.9 %fusion.17 = (bf16[256,2048]{1,0:T(8,128)(2,1)}, bf16[256,2048]{1,0:T(8,128)(2,1)}, bf16[256,2048]{1,0:T(8,128)(2,1)}, bf16[256,2048]{1,0:T(8,128)(2,1)}, bf16[2...) fusion(f32[2048]{0:T(1024)S(1)} %bitcast.44, f32[2048]{0:T(1024)S(1)} %bitcast.39, bf16[256,4096]{1,0:T(8,128)(2,1)S(1)} %bitcast.33, ...), kind=kOutput, calls=%fused_computation.31 | convolution fusion | flops 117968896 | bytes 8578048 | tf_op jit(solution)/shard_map/dot_general | solution.py:30
  88.4 17.2 %all-gather.3.cloned.1.call-done = bf16[288,4096]{1,0:T(8,128)(2,1)} async-done(((bf16[288,512]{1,0:T(8,128)(2,1)}), bf16[288,4096]{1,0:T(8,128)(2,1)}) %all-gather.3.cloned.1.call-update) | async-done | bytes 2359312 | tf_op jit(solution)/shard_map/all_gather | solution.py:75
  105.6 0.0 copy-start.7
  105.6 0.0 copy-start.8
  105.6 5.8 %fusion.12 = f32[16,288]{1,0:T(8,128)S(1)} fusion(bf16[288,4096]{1,0:T(8,128)(2,1)} %all-gather.3.cloned.1.call-done, f32[16,2048]{1,0:T(8,128)S(1)} %multiply_multiply_fusion), kind=kOutput, calls=%fused_computation.13 | convolution fusion | flops 228917248 | bytes 2508800 | tf_op jit(solution)/shard_map/dot_general | solution.py:102
  111.4 0.0 copy-start.5
  111.4 0.0 copy-start.6
  111.5 0.4 convolution_multiply_fusion.1
  111.8 0.2 sub.67
  112.1 0.2 copy.15
  112.2 0.0 copy-done.7
  112.2 0.0 copy-done.8
  112.3 0.8 copy-done.5
  113.1 0.3 copy-done.6
  113.4 21.1 %fusion.55 = (f32[768]{0:T(1024)S(1)}, f32[768,288]{0,1:T(8,128)S(1)}, f32[768,288]{0,1:T(8,128)S(1)}) fusion(f32[768,288]{0,1:T(8,128)S(1)} %bitcast.36, bf16[288,4096]{1,0:T(8,128)(2,1)S(1)} %copy-done.5, bf16[256,2048]{1,0:T(8,128)(2,1)S(1)} %copy-done.8, bf16[256,2048]{1,0:T(8,128)(2,1)} %get-tuple-element.14, bf16[256,2048]{1,0:T(8,128)(2,1)} %get-tuple-element.15, ...), kind=kOutput, calls=%fused_computation.96 | convolution fusion | flops 1850129664 | bytes 11308032 | tf_op jit(solution)/shard_map/dot_general | solution.py:100
  134.5 0.1 exponential_reduce_fusion.1
  134.7 0.5 reshape.90
  135.2 1.0 exponential_reduce_fusion
  136.2 0.7 broadcast_select_fusion
  137.0 3.5 %all-to-all-start.2 = ((f32[256,4,72]{0,2,1:T(8,128)}), f32[256,4,72]{0,2,1:T(8,128)S(1)}, u32[]{:S(2)}, u32[]{:S(2)}) async-start(f32[256,4,72]{0,2,1:T(8,128)} %broadcast_select_fusion), calls=%async_computation.2 | async-start | bytes 589824 | tf_op jit(solution)/shard_map/all_to_all | solution.py:111
  140.4 7.2 %all-gather = f32[4,1,256]{2,1,0:T(1,128)S(1)} all-gather(f32[1,1,256]{2,1,0:T(1,128)S(1)} %bitcast.45), channel_id=1, replica_groups=mesh['dom'=8,'cls'=4] {'cls'}, dimensions={0}, use_global_device_ids=true | all-gather | bytes 5120 | tf_op jit(solution)/shard_map/all_gather | solution.py:112
  147.7 0.0 all-to-all-done.2
  147.7 0.7 copy.14
  148.4 0.6 copy.17
  (13 shorter events, 0.2 us)
Async XLA Ops:
  7.2 9.7 %copy-start = (bf16[128,4096]{1,0:T(8,128)(2,1)S(1)}, bf16[128,4096]{1,0:T(8,128)(2,1)}, u32[]{:S(2)}) copy-start(bf16[128,4096]{1,0:T(8,128)(2,1)} %param.7) | copy-start | bytes 3145732
  9.6 13.6 %all-to-all-start = ((s32[8,32,1]{1,2,0:T(1,128)}), s32[8,32,1]{1,2,0:T(1,128)S(1)}, u32[]{:S(2)}, u32[]{:S(2)}) async-start(s32[8,32,1]{1,2,0:T(1,128)} %bitcast.1), calls=%async_computation | async-start | bytes 8192 | tf_op jit(solution)/shard_map/all_to_all | solution.py:94
  23.2 3.8 %copy-start.2 = (bf16[72,512]{1,0:T(8,128)(2,1)S(1)}, bf16[72,512]{1,0:T(8,128)(2,1)}, u32[]{:S(2)}) copy-start(bf16[72,512]{1,0:T(8,128)(2,1)} %param.13) | copy-start | bytes 221188
  23.2 10.3 %copy-start.4 = (s32[3,2]{0,1:T(2,128)S(1)}, s32[3,2]{0,1:T(2,128)}, u32[]{:S(2)}) copy-start(s32[3,2]{0,1:T(2,128)} %param.10) | copy-start | bytes 76
  23.2 10.7 %copy-start.1 = (f32[16,2048]{1,0:T(8,128)S(1)}, f32[16,2048]{1,0:T(8,128)}, u32[]{:S(2)}) copy-start(f32[16,2048]{1,0:T(8,128)} %param.12) | copy-start | bytes 393220
  23.2 10.7 %copy-start.3 = (f32[2048]{0:T(1024)S(1)}, f32[2048]{0:T(1024)}, u32[]{:S(2)}) copy-start(f32[2048]{0:T(1024)} %param.11) | copy-start | bytes 24580
  23.2 60.3 %all-to-all-start.1 = ((bf16[8,32,4096]{2,1,0:T(8,128)(2,1)}), bf16[8,32,4096]{2,1,0:T(8,128)(2,1)S(1)}, u32[]{:S(2)}, u32[]{:S(2)}) async-start(bf16[8,32,4096]{2,1,0:T(8,128)(2,1)} %bitcast.2), calls=%async_computation.1 | async-start | bytes 4194304 | tf_op jit(solution)/shard_map/all_to_all | solution.py:93
  27.0 78.6 %all-gather.3.cloned.1.call-start = ((), (), s32[]{:S(2)}) async-start(), calls=%async_computation.3 | async-start | bytes 2654208 | tf_op jit(solution)/shard_map/all_gather | solution.py:75
  105.6 6.6 %copy-start.7 = (bf16[256,2048]{1,0:T(8,128)(2,1)S(1)}, bf16[256,2048]{1,0:T(8,128)(2,1)}, u32[]{:S(2)}) copy-start(bf16[256,2048]{1,0:T(8,128)(2,1)} %get-tuple-element.8) | copy-start | bytes 3145732
  105.6 6.6 %copy-start.8 = (bf16[256,2048]{1,0:T(8,128)(2,1)S(1)}, bf16[256,2048]{1,0:T(8,128)(2,1)}, u32[]{:S(2)}) copy-start(bf16[256,2048]{1,0:T(8,128)(2,1)} %get-tuple-element.13) | copy-start | bytes 3145732
  111.4 1.7 %copy-start.5 = (bf16[288,4096]{1,0:T(8,128)(2,1)S(1)}, bf16[288,4096]{1,0:T(8,128)(2,1)}, u32[]{:S(2)}) copy-start(bf16[288,4096]{1,0:T(8,128)(2,1)} %all-gather.3.cloned.1.call-done) | copy-start | bytes 7077892
  111.4 1.9 %copy-start.6 = (bf16[256,2048]{1,0:T(8,128)(2,1)S(1)}, bf16[256,2048]{1,0:T(8,128)(2,1)}, u32[]{:S(2)}) copy-start(bf16[256,2048]{1,0:T(8,128)(2,1)} %get-tuple-element.7) | copy-start | bytes 3145732
  137.0 10.7 %all-to-all-start.2 = ((f32[256,4,72]{0,2,1:T(8,128)}), f32[256,4,72]{0,2,1:T(8,128)S(1)}, u32[]{:S(2)}, u32[]{:S(2)}) async-start(f32[256,4,72]{0,2,1:T(8,128)} %broadcast_select_fusion), calls=%async_computation.2 | async-start | bytes 589824 | tf_op jit(solution)/shard_map/all_to_all | solution.py:111
Sparse Core Ops, SparseCore 0:
  33.6 71.9 all-gather.2
where the time goes:
time: 156 us
  waiting for transfers between devices  69.9 us (45%)
  matrix products  35.1 us (22%)
  starting transfers between devices  14.5 us (9%)
  between operations  14.2 us (9%)
  blocking collectives  13.6 us (9%)
  local copies, waits for them, and re-layouts  4.67 us (3%)
  other arithmetic  3.82 us (2%)
    all_to_all x1, waiting for transfers between devices, shards(): lax.all_to_all(send_images, 'dom', split_axis=0, concat_axis=0, tiled=True)  48.3 us
    dot_general x1, matrix products, shards(): lax.dot_general(shifted, every_ref, contract, preferred_element_type=jnp....  21.1 us
    all_gather x1, waiting for transfers between devices, shards(): every_ref = lax.all_gather(class_rows, 'dom', axis=1, tiled=True)  17.2 us
    all_to_all x1, starting transfers between devices, shards(): lax.all_to_all(send_groups, 'dom', split_axis=0, concat_axis=0, tiled=True)  7.25 us
    all_gather x1, blocking collectives, shards(): log_norms = lax.all_gather(log_norm, 'cls', axis=0, tiled=True)  7.23 us
    all_gather x1, blocking collectives, shards(): class_rows = lax.all_gather(references, 'cls', axis=0, tiled=True)  6.4 us
    dot_general x1, matrix products, shards(): lax.dot_general(noise_terms, ref_float * ref_float, contract, precision=l...  5.8 us
    dot_general x1, matrix products, shifted_rows(): jnp.dot(group_hot, ctf_table, precision=lax.Precision.HIGHEST, preferred_...  4.88 us
  transfers between devices with their start and end apart: 4, of which 3 were waited for; matrix products, arithmetic and copies ran while one was open for 5% of the time, Pallas kernels for 0%

commit v1 on v0

v1 whole, which is shorter than its diff:
```python
import math

import jax
import jax.numpy as jnp
from jax import lax
from jax.sharding import PartitionSpec as P

SIDE = 64


def phase_tables(offsets, kept):
    freq_index = jnp.arange(kept, dtype=jnp.int32)
    half_side = SIDE // 2
    row_freq = freq_index // half_side
    col_freq = freq_index % half_side
    row_freq = jnp.where(row_freq >= half_side, row_freq - SIDE, row_freq)
    turns = jnp.mod(offsets[:, 0:1] * row_freq[None, :] + offsets[:, 1:2] * col_freq[None, :], SIDE)
    angles = turns.astype(jnp.float32) * (2.0 * math.pi / SIDE)
    return (jnp.cos(angles), jnp.sin(angles))


def shifted_rows(images, group_hot, offsets, inv_noise, ctf_table):
    kept = inv_noise.shape[0]
    cosines, sines = phase_tables(offsets, kept)
    ctf_rows = jnp.dot(
        group_hot, ctf_table, precision=lax.Precision.HIGHEST, preferred_element_type=jnp.float32
    )
    weight = inv_noise[None, :] * ctf_rows
    real_part = images[:, :kept].astype(jnp.float32)
    imag_part = images[:, kept:].astype(jnp.float32)
    pieces = []
    for shift_index in range(offsets.shape[0]):
        cosine = cosines[shift_index][None, :]
        sine = sines[shift_index][None, :]
        both = jnp.concatenate(
            [
                weight * (real_part * cosine - imag_part * sine),
                weight * (real_part * sine + imag_part * cosine),
            ],
            axis=1,
        )
        pieces.append(both.astype(jnp.bfloat16))
    return jnp.concatenate(pieces, axis=0)


def slots_of(target, dom_size, capacity):
    local_count = target.shape[0]
    target_hot = (target[:, None] == jnp.arange(dom_size, dtype=jnp.int32)[None, :]).astype(
        jnp.float32
    )
    local_index = jnp.arange(local_count, dtype=jnp.int32)
    lower = (local_index[:, None] > local_index[None, :]).astype(jnp.float32)
    earlier = jnp.dot(lower, target_hot, preferred_element_type=jnp.float32)
    position_rank = jnp.sum(earlier * target_hot, axis=1).astype(jnp.int32)
    return target * capacity + position_rank


def plain_shards(images, destinations, group_ids, offsets, inv_noise, ctf_table, references):
    dom_size = lax.axis_size("dom")
    cls_size = lax.axis_size("cls")
    local_count = images.shape[0]
    shift_count = offsets.shape[0]
    group_count = ctf_table.shape[0]
    class_count = references.shape[0]
    capacity = 2 * local_count // dom_size
    slot_count = dom_size * capacity
    class_rows = lax.all_gather(references, "cls", axis=0, tiled=True)
    every_ref = lax.all_gather(class_rows, "dom", axis=1, tiled=True)
    slot_of = slots_of(destinations[:, 0], dom_size, capacity)
    chosen = (jnp.arange(slot_count, dtype=jnp.int32)[:, None] == slot_of[None, :]).astype(
        jnp.float32
    )
    group_hot = (group_ids[:, None] == jnp.arange(group_count, dtype=jnp.int32)[None, :]).astype(
        jnp.float32
    )
    noise_ctf = inv_noise[None, :] * ctf_table * ctf_table
    noise_terms = jnp.concatenate([noise_ctf, noise_ctf], axis=1)
    shifted = shifted_rows(images, group_hot, offsets, inv_noise, ctf_table)
    contract = (((1,), (1,)), ((), ()))
    cross = lax.dot_general(shifted, every_ref, contract, preferred_element_type=jnp.float32)
    ref_float = every_ref.astype(jnp.float32)
    norms = lax.dot_general(
        noise_terms,
        ref_float * ref_float,
        contract,
        precision=lax.Precision.HIGHEST,
        preferred_element_type=jnp.float32,
    )
    selected = jnp.dot(
        group_hot, norms, precision=lax.Precision.HIGHEST, preferred_element_type=jnp.float32
    )
    scores = cross.reshape(shift_count, local_count, -1) - 0.5 * selected[None, :, :]
    row_peak = jnp.max(scores, axis=(0, 2))
    weights = jnp.exp(scores - row_peak[None, :, None])
    row_total = jnp.sum(weights, axis=(0, 2))
    log_norm = row_peak + jnp.log(row_total)
    posterior = jnp.sum(weights, axis=0) / row_total[:, None]
    posterior = posterior.reshape(local_count, cls_size, class_count)
    spread = jnp.broadcast_to(log_norm[:, None, None], (local_count, cls_size, 1))
    rows = jnp.concatenate([posterior, spread], axis=2).reshape(local_count, -1)
    slots = jnp.dot(
        chosen, rows, precision=lax.Precision.HIGHEST, preferred_element_type=jnp.float32
    )
    blocks = slots.reshape(dom_size, capacity, cls_size, class_count + 1).transpose(0, 2, 1, 3)
    blocks = blocks.reshape(dom_size * cls_size, capacity, class_count + 1)
    blocks = lax.all_to_all(blocks, ("dom", "cls"), split_axis=0, concat_axis=0, tiled=True)
    blocks = blocks.reshape(dom_size, cls_size, capacity, class_count + 1).transpose(1, 0, 2, 3)
    blocks = blocks.reshape(cls_size * slot_count, class_count + 1)
    return (blocks[:, :class_count], blocks[:, class_count])


def solution(mesh):
    return jax.shard_map(
        plain_shards,
        mesh=mesh,
        in_specs=(
            P(("dom", "cls"), None),
            P(("dom", "cls"), None),
            P(("dom", "cls")),
            P(),
            P(),
            P(),
            P("cls", "dom"),
        ),
        out_specs=(P("dom", "cls"), P("dom")),
        check_vma=False,
    )
```

time: 156 us -> 107 us (0.69)
  waiting for transfers between devices: 69.9 us -> 47.5 us
  matrix products: 35.1 us -> 12.8 us
  starting transfers between devices: 14.5 us -> 0.04 us
  blocking collectives: 13.6 us -> 27.1 us
  other arithmetic: 3.82 us -> 1.74 us
  local copies, waits for them, and re-layouts: 4.67 us -> 3.03 us
    all_to_all x3 -> x0, waiting for transfers between devices: 52.7 us -> none  [the longest x1 48.3 us: shards(): lax.all_to_all(send_images, 'dom', split_axis=0, concat_axis=0, tiled=True)]
    all_gather x1, waiting for transfers between devices: 17.2 us -> 47.5 us  [plain_shards(): every_ref = lax.all_gather(class_rows, 'dom', axis=1, tiled=True)]
    dot_general x5, matrix products: 30.2 us -> 8.89 us  [the longest x1 5.8 us: plain_shards(): lax.dot_general(noise_terms, ref_float * ref_float, contract, precision=l...]
    all_to_all x0 -> x1, blocking collectives: none -> 18.1 us  [plain_shards(): lax.all_to_all(blocks, ('dom', 'cls'), split_axis=0, concat_axis=0, tiled...]
    all_to_all x3 -> x0, starting transfers between devices: 14.4 us -> none  [the longest x1 7.25 us: shards(): lax.all_to_all(send_groups, 'dom', split_axis=0, concat_axis=0, tiled=True)]
    all_gather x2 -> x1, blocking collectives: 13.6 us -> 8.98 us  [plain_shards(): class_rows = lax.all_gather(references, 'cls', axis=0, tiled=True)]
  transfers between devices with their start and end apart: 4 -> 1, of which waited for: 3 -> 1; matrix products, arithmetic and copies ran while one was open for 5% -> 6% of each run, Pallas kernels for 0% -> 0%
where the time goes in v1:
time: 107 us; the launch traced here: 106 us
  waiting for transfers between devices  47.5 us (44%)
  blocking collectives  27.1 us (25%)
  between operations  14.2 us (13%)
  matrix products  12.8 us (12%)
  local copies, waits for them, and re-layouts  3.03 us (3%)
  other arithmetic  1.74 us (2%)
    all_gather x1, waiting for transfers between devices, plain_shards(): every_ref = lax.all_gather(class_rows, 'dom', axis=1, tiled=True)  47.5 us
    all_to_all x1, blocking collectives, plain_shards(): lax.all_to_all(blocks, ('dom', 'cls'), split_axis=0, concat_axis=0, tiled...  18.1 us
    all_gather x1, blocking collectives, plain_shards(): class_rows = lax.all_gather(references, 'cls', axis=0, tiled=True)  8.98 us
    dot_general x1, matrix products, plain_shards(): lax.dot_general(noise_terms, ref_float * ref_float, contract, precision=l...  5.8 us
    dot_general x1, matrix products, shifted_rows(): jnp.dot(group_hot, ctf_table, precision=lax.Precision.HIGHEST, preferred_...  3.89 us
  transfers between devices with their start and end apart: 1, of which 1 were waited for; matrix products, arithmetic and copies ran while one was open for 6% of the time, Pallas kernels for 0%

profile of v1, /device:TPU:0, one launch (start us, length us, event | category | flops | bytes accessed | tf_op | source)
XLA Modules:
  0.0 106.5 jit_solution(5479908822747250899)
XLA Ops:
  7.2 0.0 all-gather.2.cloned.1.call-start
  7.2 9.0 %all_gather.6 = bf16[288,512]{1,0:T(8,128)(2,1)} all-gather(bf16[72,512]{1,0:T(8,128)(2,1)} %param.13), channel_id=1, replica_groups=mesh['dom'=8,'cls'=4] {'cls'}, dimensions={0}, use_global_device_ids=true | all-gather | bytes 368640 | tf_op jit(solution)/shard_map/all_gather | solution.py:67
  16.2 0.0 all-gather.2.cloned.1.call-update
  16.3 0.9 fusion.15
  17.1 0.7 convert_add_fusion
  17.8 0.8 slice_bitcast_fusion.1
  18.6 0.3 fusion.53
  19.0 0.0 copy-start
  19.0 0.0 copy-start.1
  19.0 3.9 %fusion.18 = (bf16[128,2048]{1,0:T(8,128)(2,1)S(1)}, bf16[128,2048]{1,0:T(8,128)(2,1)S(1)}, bf16[128,2048]{1,0:T(8,128)(2,1)S(1)}, bf16[128,2048]{1,0:T(8,128)(2...) fusion(f32[2048]{0:T(1024)S(1)} %bitcast.63, f32[2048]{0:T(1024)S(1)} %bitcast.58, ...), kind=kOutput, calls=%fused_computation.33 | convolution fusion | flops 58984448 | bytes 4383232 | tf_op jit(solution)/shard_map/dot_general | solution.py:25
  22.9 0.0 copy-done
  22.9 0.0 copy-done.1
  22.9 0.0 copy-start.2
  22.9 47.5 %all-gather.2.cloned.1.call-done = bf16[288,4096]{1,0:T(8,128)(2,1)} async-done(((bf16[288,512]{1,0:T(8,128)(2,1)}), bf16[288,4096]{1,0:T(8,128)(2,1)}) %all-gather.2.cloned.1.call-update) | async-done | bytes 2359312 | tf_op jit(solution)/shard_map/all_gather | solution.py:68
  70.4 0.0 copy-start.3
  70.4 0.0 copy-start.4
  70.4 0.0 copy-start.5
  70.4 5.8 %fusion = f32[16,288]{1,0:T(8,128)S(1)} fusion(bf16[288,4096]{1,0:T(8,128)(2,1)} %all-gather.2.cloned.1.call-done, f32[16,2048]{1,0:T(8,128)S(1)} %multiply_multiply_fusion), kind=kOutput, calls=%fused_computation | convolution fusion | flops 228917248 | bytes 2508800 | tf_op jit(solution)/shard_map/dot_general | solution.py:82
  76.3 0.0 copy-done.2
  76.3 0.3 convolution_multiply_fusion.1
  76.6 0.1 sub.55
  76.7 0.0 copy-done.3
  76.7 0.0 copy-done.4
  76.7 0.0 copy-done.5
  76.8 1.4 %fusion.40 = (f32[384]{0:T(512)S(1)}, f32[384,288]{0,1:T(8,128)S(1)}) fusion(f32[36,8,3,128]{3,2,1,0:T(4,128)S(1)} %bitcast.52, bf16[288,4096]{1,0:T(8,128)(2,1)S(1)} %copy-done.3, bf16[128,2048]{1,0:T(8,128)(2,1)S(1)} %get-tuple-element.14, bf16[128,2048]{1,0:T(8,128)(2,1)S(1)} %get-tuple-element.15, bf16[128,2048]{1,0:T(8,128)(2,1)S(1)} %copy-done.4, ...), kind=kOutput, calls=%fused_computation.61 | convolution fusion | flops 925064832 | bytes 6391296 | tf_op jit(solution)/shard_map/dot_general | solution.py:80
  78.2 0.2 reshape.99
  78.4 0.5 exponential_reduce_fusion
  78.9 0.1 exponential_reduce_fusion.1
  79.2 0.4 fusion.37
  79.6 18.1 %all_to_all.5 = f32[32,32,73]{2,1,0:T(8,128)S(1)} all-to-all(f32[32,32,73]{2,1,0:T(8,128)S(1)} %bitcast.54), channel_id=1, replica_groups=mesh['dom'=8,'cls'=4] {'dom','cls'}, dimensions={0} | all-to-all | bytes 598016 | tf_op jit(solution)/shard_map/all_to_all | solution.py:106
  97.8 1.0 slice_reduce_fusion
  98.7 0.9 copy.14
  (15 shorter events, 0.2 us)
Async XLA Ops:
  7.2 63.3 %all-gather.2.cloned.1.call-start = ((), (), s32[]{:S(2)}) async-start(), calls=%async_computation.1 | async-start | bytes 2654208 | tf_op jit(solution)/shard_map/all_gather | solution.py:68
  19.0 3.9 %copy-start = (f32[16,2048]{1,0:T(8,128)S(1)}, f32[16,2048]{1,0:T(8,128)}, u32[]{:S(2)}) copy-start(f32[16,2048]{1,0:T(8,128)} %param.12) | copy-start | bytes 393220
  19.0 3.9 %copy-start.1 = (f32[2048]{0:T(1024)S(1)}, f32[2048]{0:T(1024)}, u32[]{:S(2)}) copy-start(f32[2048]{0:T(1024)} %param.11) | copy-start | bytes 24580
  22.9 53.4 %copy-start.2 = (s32[128]{0:T(128)S(1)}, s32[128]{0:T(128)}, u32[]{:S(2)}) copy-start(s32[128]{0:T(128)} %param.9) | copy-start | bytes 1540
  70.4 6.3 %copy-start.3 = (bf16[288,4096]{1,0:T(8,128)(2,1)S(1)}, bf16[288,4096]{1,0:T(8,128)(2,1)}, u32[]{:S(2)}) copy-start(bf16[288,4096]{1,0:T(8,128)(2,1)} %all-gather.2.cloned.1.call-done) | copy-start | bytes 7077892
  70.4 6.3 %copy-start.4 = (bf16[128,2048]{1,0:T(8,128)(2,1)S(1)}, bf16[128,2048]{1,0:T(8,128)(2,1)}, u32[]{:S(2)}) copy-start(bf16[128,2048]{1,0:T(8,128)(2,1)} %get-tuple-element.16) | copy-start | bytes 1572868
  70.4 6.3 %copy-start.5 = (bf16[128,2048]{1,0:T(8,128)(2,1)S(1)}, bf16[128,2048]{1,0:T(8,128)(2,1)}, u32[]{:S(2)}) copy-start(bf16[128,2048]{1,0:T(8,128)(2,1)} %get-tuple-element.17) | copy-start | bytes 1572868
Sparse Core Ops, SparseCore 0:
  16.3 54.0 all-gather.1

commit v2 on v1

--- a/solution.py
+++ b/solution.py
@@ -1,8 +1,11 @@
+import functools
 import math
 
 import jax
 import jax.numpy as jnp
 from jax import lax
+from jax.experimental import pallas as pl
+from jax.experimental.pallas import tpu as pltpu
 from jax.sharding import PartitionSpec as P
 
 SIDE = 64
@@ -109,9 +112,375 @@
     return (blocks[:, :class_count], blocks[:, class_count])
 
 
+MESH = pl.DeviceIdType.MESH
+NT_DIMS = (((1,), (1,)), ((), ()))
+
+
+def three_parts(value):
+    high = value.astype(jnp.bfloat16)
+    rest = value - high.astype(jnp.float32)
+    middle = rest.astype(jnp.bfloat16)
+    low = (rest - middle.astype(jnp.float32)).astype(jnp.bfloat16)
+    return [high, middle, low]
+
+
+def e_step_kernel(
+    dom_size,
+    cls_size,
+    offsets_ref,
+    images_ref,
+    target_ref,
+    group_ref,
+    inv_noise_ref,
+    ctf_ref,
+    refs_ref,
+    out_ref,
+    held,
+    shifted,
+    ctf_parts,
+    noise_parts,
+    phases,
+    cross,
+    norms,
+    stage,
+    send_sem,
+    recv_sem,
+    post_send,
+    post_recv,
+    own_sem,
+):
+    z_size = dom_size // 2
+    class_count, block_columns = refs_ref.shape
+    half_columns = block_columns // 2
+    padded = held.shape[3]
+    local_count = images_ref.shape[0]
+    kept = inv_noise_ref.shape[1]
+    group_count = ctf_ref.shape[0]
+    shift_count = offsets_ref.shape[0]
+    slot_count = stage.shape[1]
+    capacity = slot_count // dom_size
+    dom = lax.axis_index("dom")
+    cls = lax.axis_index("cls")
+    z, x = dom // 2, dom % 2
+    y, core = cls // 2, cls % 2
+
+    barrier = pltpu.get_barrier_semaphore()
+    partners = [
+        (lax.rem(dom + i, dom_size), lax.rem(cls + j, cls_size))
+        for i in range(dom_size)
+        for j in range(cls_size)
+        if i or j
+    ]
+    for partner in partners:
+        pl.semaphore_signal(barrier, inc=1, device_id=partner, device_id_type=MESH)
+
+    for half in range(2):
+        held[half, dom, cls, 0:class_count, :] = refs_ref[
+            :, half * half_columns : (half + 1) * half_columns
+        ]
+        held[half, dom, cls, class_count:padded, :] = jnp.zeros(
+            (padded - class_count, half_columns), jnp.bfloat16
+        )
+    pl.semaphore_wait(barrier, len(partners))
+
+    sends = []
+
+    def block_copy(half, block_dom, block_cls, device, index):
+        block = held.at[half, block_dom, block_cls]
+        return pltpu.make_async_remote_copy(
+            src_ref=block,
+            dst_ref=block,
+            send_sem=send_sem.at[index],
+            recv_sem=recv_sem.at[half, block_dom, block_cls],
+            device_id=device,
+            device_id_type=MESH,
+        )
+
+    def send(half, block_dom, block_cls, device):
+        copy = block_copy(half, block_dom, block_cls, device, len(sends))
+        copy.start()
+        sends.append(copy)
+
+    def arrived(half, block_dom, block_cls):
+        block_copy(half, block_dom, block_cls, over_core, 0).wait_recv()
+
+    over_x = (z * 2 + (1 - x), cls)
+    over_y = (dom, (1 - y) * 2 + core)
+    over_core = (dom, y * 2 + (1 - core))
+    first = [over_x, over_y]
+    last = [over_y, over_x]
+
+    for half in range(2):
+        send(half, dom, cls, first[half])
+    for step in range(1, z_size):
+        for half in range(2):
+            send(half, dom, cls, (lax.rem(z + step, z_size) * 2 + x, cls))
+    for half in range(2):
+        send(half, dom, cls, last[half])
+        send(half, dom, cls, over_core)
+
+    freq = lax.broadcasted_iota(jnp.int32, (1, kept), 1)
+    half_side = SIDE // 2
+    row_freq = freq // half_side
+    col_freq = freq % half_side
+    row_freq = jnp.where(row_freq >= half_side, row_freq - SIDE, row_freq)
+    for t in range(shift_count):
+        turns = (offsets_ref[t, 0] * row_freq + offsets_ref[t, 1] * col_freq) & (SIDE - 1)
+        angles = turns.astype(jnp.float32) * (2.0 * math.pi / SIDE)
+        phases[2 * t : 2 * t + 1, :] = jnp.cos(angles)
+        phases[2 * t + 1 : 2 * t + 2, :] = jnp.sin(angles)
+    ctf = ctf_ref[...]
+    noise_terms = inv_noise_ref[...] * ctf * ctf
+    for index, part in enumerate(three_parts(ctf)):
+        ctf_parts[index * group_count : (index + 1) * group_count, :] = part
+    for index, part in enumerate(three_parts(noise_terms)):
+        noise_parts[index * group_count : (index + 1) * group_count, :] = part
+    square = (local_count, local_count)
+    sub = lax.broadcasted_iota(jnp.int32, square, 0)
+    lane = lax.broadcasted_iota(jnp.int32, square, 1)
+    group_row = group_ref[...]
+    group_col = jnp.sum(jnp.where(sub == lane, group_row, 0), axis=1, keepdims=True)
+    part_lane = lax.broadcasted_iota(jnp.int32, (local_count, 3 * group_count), 1)
+    group_hot = jnp.where(part_lane % group_count == group_col, 1.0, 0.0).astype(jnp.bfloat16)
+
+    chunk = kept // z_size
+
+    def shift_chunk(step):
+        low = step * chunk
+        columns = slice(low, low + chunk)
+        imag_columns = slice(kept + low, kept + low + chunk)
+        weight = inv_noise_ref[:, columns] * jnp.dot(
+            group_hot, ctf_parts[:, columns], preferred_element_type=jnp.float32
+        )
+        real_part = images_ref[:, columns].astype(jnp.float32)
+        imag_part = images_ref[:, imag_columns].astype(jnp.float32)
+        for t in range(shift_count):
+            cosine = phases[2 * t : 2 * t + 1, columns]
+            sine = phases[2 * t + 1 : 2 * t + 2, columns]
+            rows = slice(t * local_count, (t + 1) * local_count)
+            shifted[rows, columns] = (
+                weight * (real_part * cosine - imag_part * sine)
+            ).astype(jnp.bfloat16)
+            shifted[rows, imag_columns] = (
+                weight * (real_part * sine + imag_part * cosine)
+            ).astype(jnp.bfloat16)
+
+    z_order = [0, 1, z_size - 1] + list(range(2, z_size - 1))
+    z_order = z_order[:z_size]
+    shift_chunk(0)
+    for count, step in enumerate(z_order[1:]):
+        block = lax.rem(z + step, z_size) * 2 + x
+        for half in range(2):
+            arrived(half, block, cls)
+            send(half, block, cls, first[half])
+        for half in range(2):
+            send(half, block, cls, last[half])
+            send(half, block, cls, over_core)
+        shift_chunk(count + 1)
+
+    for step in z_order:
+        block_z = lax.rem(z + step, z_size)
+        for half in range(2):
+            block = (block_z * 2 + (1 - x), cls) if half == 0 else (block_z * 2 + x, over_y[1])
+            arrived(half, *block)
+            send(half, *block, last[half])
+            send(half, *block, over_core)
+
+    cross[...] = jnp.zeros_like(cross)
+    norms[...] = jnp.zeros_like(norms)
+
+    def add_block(half, block_dom):
+        sibling = lax.rem(core + 1, 2)
+        arrived(half, block_dom, sibling)
+        arrived(half, block_dom, 2 + sibling)
+        rows = held[half, block_dom].reshape(cls_size * padded, half_columns)
+        low = pl.multiple_of(block_dom * block_columns + half * half_columns, half_columns)
+        cross[...] += lax.dot_general(
+            rows, shifted[:, pl.ds(low, half_columns)], NT_DIMS, preferred_element_type=jnp.float32
+        )
+        wide = rows.astype(jnp.float32)
+        squares = wide * wide
+        high = squares.astype(jnp.bfloat16)
+        rest = (squares - high.astype(jnp.float32)).astype(jnp.bfloat16)
+        low = pl.multiple_of(lax.rem(low, kept), half_columns)
+        noise = noise_parts[:, pl.ds(low, half_columns)]
+        norms[...] += lax.dot_general(
+            high, noise, NT_DIMS, preferred_element_type=jnp.float32
+        ) + lax.dot_general(rest, noise, NT_DIMS, preferred_element_type=jnp.float32)
+
+    waiting = []
+    for near in range(2):
+        for step in z_order:
+            block_z = lax.rem(z + step, z_size)
+            for half in range(2):
+                if half == 0:
+                    block_x = x if near == 0 else 1 - x
+                    block_dom = block_z * 2 + block_x
+                    block = (block_dom, over_y[1])
+                else:
+                    block_dom = block_z * 2 + (1 - x)
+                    block = (block_dom, cls if near == 0 else over_y[1])
+                arrived(half, *block)
+                send(half, *block, over_core)
+                if half == 0:
+                    waiting.append((0, block_dom))
+                elif near == 0:
+                    waiting.append((1, block_z * 2 + x))
+                else:
+                    waiting.append((1, block_dom))
+                if len(waiting) > 2:
+                    add_block(*waiting.pop(0))
+    for item in waiting:
+        add_block(*item)
+
+    rows_all = cls_size * padded
+    hot_rows = lax.broadcasted_iota(jnp.int32, (9 * group_count, local_count), 0)
+    hot_groups = jnp.where(hot_rows % group_count == group_row, 1.0, 0.0).astype(jnp.bfloat16)
+    selected = 0.5 * jnp.dot(
+        jnp.concatenate(three_parts(norms[...]), axis=1),
+        hot_groups,
+        preferred_element_type=jnp.float32,
+    )
+    row = lax.broadcasted_iota(jnp.int32, (rows_all, local_count), 0) % padded
+    real_row = row < class_count
+    scores = []
+    for t in range(shift_count):
+        value = cross[:, t * local_count : (t + 1) * local_count] - selected
+        scores.append(jnp.where(real_row, value, -jnp.inf))
+    peak = functools.reduce(jnp.maximum, scores)
+    peak = jnp.max(peak, axis=0, keepdims=True)
+    weights = functools.reduce(jnp.add, [jnp.exp(value - peak) for value in scores])
+    total = jnp.sum(weights, axis=0, keepdims=True)
+    log_norm = peak + jnp.log(total)
+    table = jnp.where(row == class_count, log_norm, weights / total)
+    table = jnp.concatenate(three_parts(table), axis=1)
+
+    target_col = target_ref[...]
+    target_row = jnp.sum(jnp.where(sub == lane, target_col, 0), axis=0, keepdims=True)
+    ahead = (target_col == target_row) & (sub < lane)
+    rank = jnp.sum(jnp.where(ahead, 1, 0), axis=0, keepdims=True)
+    slot_of = target_row * capacity + rank
+    slot = lax.broadcasted_iota(jnp.int32, (slot_count, local_count), 0)
+    hot = jnp.where(slot == slot_of, 1.0, 0.0).astype(jnp.bfloat16)
+    hot = jnp.concatenate([hot, hot, hot], axis=1)
+    for block in range(cls_size):
+        stage[block, :, 0:padded] = lax.dot_general(
+            hot,
+            table[block * padded : (block + 1) * padded, :],
+            NT_DIMS,
+            preferred_element_type=jnp.float32,
+        )
+
+    def landing(source_dom, source_cls):
+        start = pl.multiple_of(source_cls * slot_count + source_dom * capacity, capacity)
+        return out_ref.at[pl.ds(start, capacity), :]
+
+    def source(to_dom, to_cls):
+        start = pl.multiple_of(to_dom * capacity, capacity)
+        return stage.at[to_cls, pl.ds(start, capacity), :]
+
+    posts = []
+    for index, (to_dom, to_cls) in enumerate(partners):
+        copy = pltpu.make_async_remote_copy(
+            src_ref=source(to_dom, to_cls),
+            dst_ref=landing(dom, cls),
+            send_sem=post_send.at[index],
+            recv_sem=post_recv.at[dom, cls],
+            device_id=(to_dom, to_cls),
+            device_id_type=MESH,
+        )
+        copy.start()
+        posts.append(copy)
+    own = pltpu.make_async_copy(source(dom, cls), landing(dom, cls), own_sem)
+    own.start()
+    for copy in sends:
+        copy.wait_send()
+    for copy in posts:
+        copy.wait_send()
+    own.wait()
+    for from_dom, from_cls in partners:
+        pltpu.make_async_remote_copy(
+            src_ref=source(from_dom, from_cls),
+            dst_ref=landing(from_dom, from_cls),
+            send_sem=post_send.at[0],
+            recv_sem=post_recv.at[from_dom, from_cls],
+            device_id=(from_dom, from_cls),
+            device_id_type=MESH,
+        ).wait_recv()
+
+
+def kernel_shards(images, destinations, group_ids, offsets, inv_noise, ctf_table, references):
+    dom_size = lax.axis_size("dom")
+    cls_size = lax.axis_size("cls")
+    local_count, columns = images.shape
+    kept = inv_noise.shape[0]
+    group_count = ctf_table.shape[0]
+    shift_count = offsets.shape[0]
+    class_count, block_columns = references.shape
+    slot_count = 2 * local_count
+    padded = -(-(class_count + 1) // 16) * 16
+    device_count = dom_size * cls_size
+    vmem = pl.BlockSpec(memory_space=pltpu.VMEM)
+    out = pl.pallas_call(
+        functools.partial(e_step_kernel, dom_size, cls_size),
+        out_shape=jax.ShapeDtypeStruct((cls_size * slot_count, 128), jnp.float32),
+        in_specs=[pl.BlockSpec(memory_space=pltpu.SMEM)] + [vmem] * 6,
+        out_specs=pl.BlockSpec(memory_space=pl.ANY),
+        scratch_shapes=[
+            pltpu.VMEM((2, dom_size, cls_size, padded, block_columns // 2), jnp.bfloat16),
+            pltpu.VMEM((shift_count * local_count, columns), jnp.bfloat16),
+            pltpu.VMEM((3 * group_count, kept), jnp.bfloat16),
+            pltpu.VMEM((3 * group_count, kept), jnp.bfloat16),
+            pltpu.VMEM((2 * shift_count, kept), jnp.float32),
+            pltpu.VMEM((cls_size * padded, shift_count * local_count), jnp.float32),
+            pltpu.VMEM((cls_size * padded, 3 * group_count), jnp.float32),
+            pltpu.VMEM((cls_size, slot_count, 128), jnp.float32),
+            pltpu.SemaphoreType.DMA((2 * device_count + dom_size,)),
+            pltpu.SemaphoreType.DMA((2, dom_size, cls_size)),
+            pltpu.SemaphoreType.DMA((device_count,)),
+            pltpu.SemaphoreType.DMA((dom_size, cls_size)),
+            pltpu.SemaphoreType.DMA,
+        ],
+        compiler_params=pltpu.CompilerParams(
+            collective_id=0, has_side_effects=True, vmem_limit_bytes=40 * 1024 * 1024
+        ),
+    )(
+        offsets,
+        images,
+        destinations,
+        group_ids[None, :],
+        inv_noise[None, :],
+        ctf_table,
+        references,
+    )
+    return (out[:, :class_count], out[:, class_count])
+
+
+def fits_kernel(mesh, images, references):
+    dom_size, cls_size = mesh.shape["dom"], mesh.shape["cls"]
+    local_count = images.shape[0] // (dom_size * cls_size)
+    block_columns = references.shape[1] // dom_size
+    return (
+        cls_size == 4
+        and dom_size % 2 == 0
+        and local_count == 128
+        and 2 * local_count // dom_size % 8 == 0
+        and block_columns % 256 == 0
+        and references.shape[0] // cls_size < 128
+    )
+
+
 def solution(mesh):
+    def e_step(*arrays):
+        shards = kernel_shards if fits_kernel(mesh, arrays[0], arrays[-1]) else plain_shards
+        return mapped(mesh, shards)(*arrays)
+
+    return e_step
+
+
+def mapped(mesh, shards):
     return jax.shard_map(
-        plain_shards,
+        shards,
         mesh=mesh,
         in_specs=(
             P(("dom", "cls"), None),

time: 107 us -> 52.3 us (0.49)
  the two profiles are of different devices: /device:TPU:0 before, /device:TPU:27 now
where the time goes in v2:
time: 52.3 us; the launch traced here: 52 us
  Pallas kernels  44.4 us (85%)
  local copies, waits for them, and re-layouts  6.89 us (13%)
  between operations  0.65 us (1%)
    pallas_call x1, Pallas kernels, kernel_shards(): pl.pallas_call(functools.partial(e_step_kernel, dom_size, cls_size), out_...  44.4 us
    unnamed x17, local copies, waits for them, and re-layouts  5.94 us

profile of v2, /device:TPU:27, one launch (start us, length us, event | category | flops | bytes accessed | tf_op | source)
XLA Modules:
  0.0 52.0 jit_solution(18148653564450673947)
XLA Ops:
  0.6 0.0 copy-start.5
  0.6 0.7 %copy-done.5 = s32[3,2]{0,1:T(2,128)S(1)} copy-done((s32[3,2]{0,1:T(2,128)S(1)}, s32[3,2]{0,1:T(2,128)}, u32[]{:S(2)}) %copy-start.5) | copy-done | bytes 48
  1.3 0.0 copy-start.6
  1.3 0.1 copy.12.offsets_ref
  1.4 0.6 %copy-done.6 = s32[128,1]{0,1:T(1,128)S(1)} copy-done((s32[128,1]{0,1:T(1,128)S(1)}, s32[128,1]{0,1:T(1,128)}, u32[]{:S(2)}) %copy-start.6) | copy-done | bytes 536
  2.0 0.0 copy-start.3
  2.0 0.0 copy-start.4
  2.0 0.1 copy.13.target_ref
  2.1 0.6 %copy-done.3 = f32[2048]{0:T(1024)S(1)} copy-done((f32[2048]{0:T(1024)S(1)}, f32[2048]{0:T(1024)}, u32[]{:S(2)}) %copy-start.3) | copy-done | bytes 8216
  2.7 0.0 copy-done.4
  2.7 0.0 copy-start
  2.7 1.2 %copy-done = bf16[128,4096]{1,0:T(8,128)(2,1)S(1)} copy-done((bf16[128,4096]{1,0:T(8,128)(2,1)S(1)}, bf16[128,4096]{1,0:T(8,128)(2,1)}, u32[]{:S(2)}) %copy-start) | copy-done | bytes 1048600
  3.9 0.0 copy-start.1
  3.9 0.9 %copy-done.1 = f32[16,2048]{1,0:T(8,128)S(1)} copy-done((f32[16,2048]{1,0:T(8,128)S(1)}, f32[16,2048]{1,0:T(8,128)}, u32[]{:S(2)}) %copy-start.1) | copy-done | bytes 131096
  4.8 0.0 copy-start.2
  4.8 0.9 %copy-done.2 = bf16[72,512]{1,0:T(8,128)(2,1)S(1)} copy-done((bf16[72,512]{1,0:T(8,128)(2,1)S(1)}, bf16[72,512]{1,0:T(8,128)(2,1)}, u32[]{:S(2)}) %copy-start.2) | copy-done | bytes 73752
  5.7 44.4 %shard_map.86 = f32[1024,128]{1,0:T(8,128)S(1)} custom-call(s32[3,2]{1,0:T(4,128)S(1)} %copy.12.offsets_ref, bf16[128,4096]{1,0:T(8,128)(2,1)S(1)} %copy-done, s32[128,1]{1,0:T(8,128)S(1)} %copy.13.target_ref, s32[1,128]{1,0:T(1,128)S(1)} %bitcast.5, f32[1,2048]{1,0:T(1,128)S(1)} %bitcast.4, f32[16,2048]{1,0:T(8,128)S(1)} %copy-done.1, ...), custom_call_target="tpu_custom_call" | custom-call | tf_op jit(solution)/shard_map/pallas_call | solution.py:424
  50.1 1.0 %slice_reduce_fusion = f32[1024]{0:T(1024)} fusion(f32[1024,128]{1,0:T(8,128)S(1)} %shard_map.86), kind=kLoop, calls=%fused_computation | loop fusion | bytes 8192 | tf_op jit(solution)/shard_map/slice | solution.py:456
  51.1 0.9 %copy.14 = f32[1024,72]{0,1:T(8,128)} copy(f32[1024,72]{1,0:T(8,128)S(1)} %bitcast.3) | data formatting | bytes 589824
Async XLA Ops:
  0.6 0.7 %copy-start.5 = (s32[3,2]{0,1:T(2,128)S(1)}, s32[3,2]{0,1:T(2,128)}, u32[]{:S(2)}) copy-start(s32[3,2]{0,1:T(2,128)} %param.10) | copy-start | bytes 76
  1.3 0.7 %copy-start.6 = (s32[128,1]{0,1:T(1,128)S(1)}, s32[128,1]{0,1:T(1,128)}, u32[]{:S(2)}) copy-start(s32[128,1]{0,1:T(1,128)} %param.8) | copy-start | bytes 1540
  2.0 0.7 %copy-start.3 = (f32[2048]{0:T(1024)S(1)}, f32[2048]{0:T(1024)}, u32[]{:S(2)}) copy-start(f32[2048]{0:T(1024)} %param.11) | copy-start | bytes 24580
  2.0 0.7 %copy-start.4 = (s32[128]{0:T(128)S(1)}, s32[128]{0:T(128)}, u32[]{:S(2)}) copy-start(s32[128]{0:T(128)} %param.9) | copy-start | bytes 1540
  2.7 1.2 %copy-start = (bf16[128,4096]{1,0:T(8,128)(2,1)S(1)}, bf16[128,4096]{1,0:T(8,128)(2,1)}, u32[]{:S(2)}) copy-start(bf16[128,4096]{1,0:T(8,128)(2,1)} %images_ref.1) | copy-start | bytes 3145732
  3.9 0.9 %copy-start.1 = (f32[16,2048]{1,0:T(8,128)S(1)}, f32[16,2048]{1,0:T(8,128)}, u32[]{:S(2)}) copy-start(f32[16,2048]{1,0:T(8,128)} %ctf_ref.1) | copy-start | bytes 393220
  4.8 0.9 %copy-start.2 = (bf16[72,512]{1,0:T(8,128)(2,1)S(1)}, bf16[72,512]{1,0:T(8,128)(2,1)}, u32[]{:S(2)}) copy-start(bf16[72,512]{1,0:T(8,128)(2,1)} %refs_ref.1) | copy-start | bytes 221188

commit v3 on v2

--- a/solution.py
+++ b/solution.py
@@ -124,30 +124,60 @@
     return [high, middle, low]
 
 
+def quarter_turns(turns):
+    quarter, eighth = SIDE // 4, SIDE // 8
+    quadrant = (turns + eighth) // quarter
+    angle = (turns - quadrant * quarter).astype(jnp.float32) * (2.0 * math.pi / SIDE)
+    square = angle * angle
+    sine = 1.0 / 362880.0
+    for term in (-1.0 / 5040.0, 1.0 / 120.0, -1.0 / 6.0, 1.0):
+        sine = sine * square + term
+    sine = sine * angle
+    cosine = -1.0 / 3628800.0
+    for term in (1.0 / 40320.0, -1.0 / 720.0, 1.0 / 24.0, -0.5, 1.0):
+        cosine = cosine * square + term
+    quadrant = quadrant & 3
+    odd = (quadrant & 1) == 1
+    first = jnp.where(odd, sine, cosine)
+    second = jnp.where(odd, cosine, sine)
+    return (
+        jnp.where((quadrant == 1) | (quadrant == 2), -first, first),
+        jnp.where(quadrant >= 2, -second, second),
+    )
+
+
 def e_step_kernel(
     dom_size,
     cls_size,
     offsets_ref,
-    images_ref,
+    images_hbm,
     target_ref,
     group_ref,
+    inv_noise_hbm,
+    ctf_hbm,
+    refs_hbm,
+    out_ref,
+    log_ref,
+    images_ref,
     inv_noise_ref,
     ctf_ref,
     refs_ref,
-    out_ref,
     held,
     shifted,
     ctf_parts,
-    noise_parts,
-    phases,
+    cosines,
+    sines,
     cross,
     norms,
+    slot_hot,
+    group_hot_rows,
     stage,
+    landed,
+    load_sem,
     send_sem,
     recv_sem,
     post_send,
     post_recv,
-    own_sem,
 ):
     z_size = dom_size // 2
     class_count, block_columns = refs_ref.shape
@@ -156,31 +186,71 @@
     local_count = images_ref.shape[0]
     kept = inv_noise_ref.shape[1]
     group_count = ctf_ref.shape[0]
-    shift_count = offsets_ref.shape[0]
-    slot_count = stage.shape[1]
+    shift_count = offsets_ref.shape[1]
+    slot_count = slot_hot.shape[0]
     capacity = slot_count // dom_size
+    piece_rows, lanes = stage.shape[2:]
+    group_size = lanes // capacity
+    pieces = group_size - 1
     dom = lax.axis_index("dom")
     cls = lax.axis_index("cls")
     z, x = dom // 2, dom % 2
     y, core = cls // 2, cls % 2
 
+    loads = [
+        pltpu.make_async_copy(source, place, load_sem.at[index])
+        for index, (source, place) in enumerate(
+            [
+                (refs_hbm, refs_ref),
+                (ctf_hbm, ctf_ref),
+                (inv_noise_hbm, inv_noise_ref),
+                (images_hbm, images_ref),
+            ]
+        )
+    ]
+    for load in loads:
+        load.start()
     barrier = pltpu.get_barrier_semaphore()
     partners = [
         (lax.rem(dom + i, dom_size), lax.rem(cls + j, cls_size))
-        for i in range(dom_size)
+        for i in sorted(range(dom_size), key=lambda i: (abs(i - dom_size // 2), i))
         for j in range(cls_size)
         if i or j
     ]
     for partner in partners:
         pl.semaphore_signal(barrier, inc=1, device_id=partner, device_id_type=MESH)
 
+    for load in loads[:3]:
+        load.wait()
+    wide = refs_ref[...].astype(jnp.float32)
+    squares = jnp.concatenate(
+        [wide * wide, jnp.zeros((padded - class_count, block_columns), jnp.float32)], axis=0
+    )
+    high = squares.astype(jnp.bfloat16)
+    rest = (squares - high.astype(jnp.float32)).astype(jnp.bfloat16)
+    low = pl.multiple_of(lax.rem(dom * block_columns, kept), block_columns)
+    own_ctf = ctf_ref[:, pl.ds(low, block_columns)]
+    noise_terms = inv_noise_ref[:, pl.ds(low, block_columns)] * own_ctf * own_ctf
+    sums = lax.dot_general(
+        jnp.concatenate(three_parts(noise_terms), axis=0),
+        jnp.concatenate([high, rest], axis=0),
+        NT_DIMS,
+        preferred_element_type=jnp.float32,
+    )
+    sums = sums[:, :padded] + sums[:, padded:]
+    own_norms = (
+        sums[:group_count] + sums[group_count : 2 * group_count] + sums[2 * group_count :]
+    )
+    tail = jnp.concatenate(
+        [part.astype(jnp.float32) for part in three_parts(own_norms)]
+        + [jnp.zeros((group_count, half_columns - 3 * padded), jnp.float32)],
+        axis=1,
+    )
     for half in range(2):
-        held[half, dom, cls, 0:class_count, :] = refs_ref[
-            :, half * half_columns : (half + 1) * half_columns
-        ]
-        held[half, dom, cls, class_count:padded, :] = jnp.zeros(
-            (padded - class_count, half_columns), jnp.bfloat16
-        )
+        rows = wide[:, half * half_columns : (half + 1) * half_columns]
+        extra = padded - class_count
+        block = jnp.concatenate([rows, tail[half * extra : (half + 1) * extra]], axis=0)
+        held[half, dom, cls] = block.astype(jnp.bfloat16)
     pl.semaphore_wait(barrier, len(partners))
 
     sends = []
@@ -219,22 +289,20 @@
         send(half, dom, cls, last[half])
         send(half, dom, cls, over_core)
 
-    freq = lax.broadcasted_iota(jnp.int32, (1, kept), 1)
+    table_shape = (cosines.shape[0], kept)
+    freq = lax.broadcasted_iota(jnp.int32, table_shape, 1)
+    shift_row = lax.broadcasted_iota(jnp.int32, table_shape, 0)
     half_side = SIDE // 2
     row_freq = freq // half_side
     col_freq = freq % half_side
     row_freq = jnp.where(row_freq >= half_side, row_freq - SIDE, row_freq)
+    turns = jnp.zeros(table_shape, jnp.int32)
     for t in range(shift_count):
-        turns = (offsets_ref[t, 0] * row_freq + offsets_ref[t, 1] * col_freq) & (SIDE - 1)
-        angles = turns.astype(jnp.float32) * (2.0 * math.pi / SIDE)
-        phases[2 * t : 2 * t + 1, :] = jnp.cos(angles)
-        phases[2 * t + 1 : 2 * t + 2, :] = jnp.sin(angles)
-    ctf = ctf_ref[...]
-    noise_terms = inv_noise_ref[...] * ctf * ctf
-    for index, part in enumerate(three_parts(ctf)):
+        turn = offsets_ref[0, t] * row_freq + offsets_ref[1, t] * col_freq
+        turns = jnp.where(shift_row == t, turn & (SIDE - 1), turns)
+    cosines[...], sines[...] = quarter_turns(turns)
+    for index, part in enumerate(three_parts(ctf_ref[...])):
         ctf_parts[index * group_count : (index + 1) * group_count, :] = part
-    for index, part in enumerate(three_parts(noise_terms)):
-        noise_parts[index * group_count : (index + 1) * group_count, :] = part
     square = (local_count, local_count)
     sub = lax.broadcasted_iota(jnp.int32, square, 0)
     lane = lax.broadcasted_iota(jnp.int32, square, 1)
@@ -255,8 +323,8 @@
         real_part = images_ref[:, columns].astype(jnp.float32)
         imag_part = images_ref[:, imag_columns].astype(jnp.float32)
         for t in range(shift_count):
-            cosine = phases[2 * t : 2 * t + 1, columns]
-            sine = phases[2 * t + 1 : 2 * t + 2, columns]
+            cosine = cosines[t : t + 1, columns]
+            sine = sines[t : t + 1, columns]
             rows = slice(t * local_count, (t + 1) * local_count)
             shifted[rows, columns] = (
                 weight * (real_part * cosine - imag_part * sine)
@@ -267,6 +335,7 @@
 
     z_order = [0, 1, z_size - 1] + list(range(2, z_size - 1))
     z_order = z_order[:z_size]
+    loads[3].wait()
     shift_chunk(0)
     for count, step in enumerate(z_order[1:]):
         block = lax.rem(z + step, z_size) * 2 + x
@@ -278,6 +347,22 @@
             send(half, block, cls, over_core)
         shift_chunk(count + 1)
 
+    hot_rows = lax.broadcasted_iota(jnp.int32, group_hot_rows.shape, 0)
+    group_hot_rows[...] = jnp.where(hot_rows % group_count == group_row, 1.0, 0.0).astype(
+        jnp.bfloat16
+    )
+    target_row = target_ref[...]
+    target_col = jnp.sum(jnp.where(sub == lane, target_row, 0), axis=1, keepdims=True)
+    ahead = (target_col == target_row) & (sub < lane)
+    rank = jnp.sum(jnp.where(ahead, 1, 0), axis=0, keepdims=True)
+    slot_of = target_row * capacity + rank
+    slot = lax.broadcasted_iota(jnp.int32, (slot_count, local_count), 0)
+    hot = jnp.where(slot == slot_of, 1.0, 0.0).astype(jnp.bfloat16)
+    for index in range(3):
+        slot_hot[:, index * local_count : (index + 1) * local_count] = hot
+    cross[...] = jnp.zeros_like(cross)
+    norms[...] = jnp.zeros_like(norms)
+
     for step in z_order:
         block_z = lax.rem(z + step, z_size)
         for half in range(2):
@@ -286,62 +371,57 @@
             send(half, *block, last[half])
             send(half, *block, over_core)
 
-    cross[...] = jnp.zeros_like(cross)
-    norms[...] = jnp.zeros_like(norms)
-
-    def add_block(half, block_dom):
-        sibling = lax.rem(core + 1, 2)
-        arrived(half, block_dom, sibling)
-        arrived(half, block_dom, 2 + sibling)
-        rows = held[half, block_dom].reshape(cls_size * padded, half_columns)
-        low = pl.multiple_of(block_dom * block_columns + half * half_columns, half_columns)
+    sibling = 1 - core
+
+    def add_block(block_dom):
+        for half in range(2):
+            arrived(half, block_dom, sibling)
+            arrived(half, block_dom, 2 + sibling)
+        rows = jnp.concatenate(
+            [held[half, block_dom].reshape(cls_size * padded, half_columns) for half in range(2)],
+            axis=1,
+        )
+        low = pl.multiple_of(block_dom * block_columns, block_columns)
         cross[...] += lax.dot_general(
-            rows, shifted[:, pl.ds(low, half_columns)], NT_DIMS, preferred_element_type=jnp.float32
-        )
-        wide = rows.astype(jnp.float32)
-        squares = wide * wide
-        high = squares.astype(jnp.bfloat16)
-        rest = (squares - high.astype(jnp.float32)).astype(jnp.bfloat16)
-        low = pl.multiple_of(lax.rem(low, kept), half_columns)
-        noise = noise_parts[:, pl.ds(low, half_columns)]
-        norms[...] += lax.dot_general(
-            high, noise, NT_DIMS, preferred_element_type=jnp.float32
-        ) + lax.dot_general(rest, noise, NT_DIMS, preferred_element_type=jnp.float32)
+            rows, shifted[:, pl.ds(low, block_columns)], NT_DIMS, preferred_element_type=jnp.float32
+        )
+        for half in range(2):
+            last_rows = held[half, block_dom, :, padded - 16 : padded, :].astype(jnp.float32)
+            norms[half] += last_rows[:, 8:16, :]
 
     waiting = []
     for near in range(2):
         for step in z_order:
             block_z = lax.rem(z + step, z_size)
+            block_dom = block_z * 2 + (x if near == 0 else 1 - x)
+            far_block = block_z * 2 + (1 - x)
             for half in range(2):
                 if half == 0:
-                    block_x = x if near == 0 else 1 - x
-                    block_dom = block_z * 2 + block_x
                     block = (block_dom, over_y[1])
                 else:
-                    block_dom = block_z * 2 + (1 - x)
-                    block = (block_dom, cls if near == 0 else over_y[1])
+                    block = (far_block, cls if near == 0 else over_y[1])
                 arrived(half, *block)
                 send(half, *block, over_core)
-                if half == 0:
-                    waiting.append((0, block_dom))
-                elif near == 0:
-                    waiting.append((1, block_z * 2 + x))
-                else:
-                    waiting.append((1, block_dom))
-                if len(waiting) > 2:
-                    add_block(*waiting.pop(0))
+            waiting.append(block_dom)
+            if len(waiting) > 1:
+                add_block(waiting.pop(0))
     for item in waiting:
-        add_block(*item)
-
-    rows_all = cls_size * padded
-    hot_rows = lax.broadcasted_iota(jnp.int32, (9 * group_count, local_count), 0)
-    hot_groups = jnp.where(hot_rows % group_count == group_row, 1.0, 0.0).astype(jnp.bfloat16)
-    selected = 0.5 * jnp.dot(
-        jnp.concatenate(three_parts(norms[...]), axis=1),
-        hot_groups,
-        preferred_element_type=jnp.float32,
-    )
-    row = lax.broadcasted_iota(jnp.int32, (rows_all, local_count), 0) % padded
+        add_block(item)
+
+    selected = []
+    for block in range(cls_size):
+        both = jnp.concatenate([norms[0, block], norms[1, block]], axis=0)
+        total_norm = sum(both[:, p * padded : (p + 1) * padded] for p in range(3))
+        selected.append(
+            lax.dot_general(
+                jnp.concatenate(three_parts(total_norm), axis=0),
+                group_hot_rows[...],
+                (((0,), (0,)), ((), ())),
+                preferred_element_type=jnp.float32,
+            )
+        )
+    selected = 0.5 * jnp.concatenate(selected, axis=0)
+    row = lax.broadcasted_iota(jnp.int32, (cls_size * padded, local_count), 0) % padded
     real_row = row < class_count
     scores = []
     for t in range(shift_count):
@@ -353,60 +433,74 @@
     total = jnp.sum(weights, axis=0, keepdims=True)
     log_norm = peak + jnp.log(total)
     table = jnp.where(row == class_count, log_norm, weights / total)
-    table = jnp.concatenate(three_parts(table), axis=1)
-
-    target_col = target_ref[...]
-    target_row = jnp.sum(jnp.where(sub == lane, target_col, 0), axis=0, keepdims=True)
-    ahead = (target_col == target_row) & (sub < lane)
-    rank = jnp.sum(jnp.where(ahead, 1, 0), axis=0, keepdims=True)
-    slot_of = target_row * capacity + rank
-    slot = lax.broadcasted_iota(jnp.int32, (slot_count, local_count), 0)
-    hot = jnp.where(slot == slot_of, 1.0, 0.0).astype(jnp.bfloat16)
-    hot = jnp.concatenate([hot, hot, hot], axis=1)
+
+    slots = lax.dot_general(
+        jnp.concatenate(three_parts(table), axis=1),
+        slot_hot[...],
+        NT_DIMS,
+        preferred_element_type=jnp.float32,
+    )
+    lane_group = lax.broadcasted_iota(jnp.int32, (piece_rows, lanes), 1) // capacity
+
+    def turned(value, groups):
+        amount = groups % group_size * capacity
+        return pltpu.roll(value, amount, 1) if amount else value
+
     for block in range(cls_size):
-        stage[block, :, 0:padded] = lax.dot_general(
-            hot,
-            table[block * padded : (block + 1) * padded, :],
-            NT_DIMS,
-            preferred_element_type=jnp.float32,
-        )
-
-    def landing(source_dom, source_cls):
-        start = pl.multiple_of(source_cls * slot_count + source_dom * capacity, capacity)
-        return out_ref.at[pl.ds(start, capacity), :]
-
-    def source(to_dom, to_cls):
-        start = pl.multiple_of(to_dom * capacity, capacity)
-        return stage.at[to_cls, pl.ds(start, capacity), :]
+        part = slots[block * padded : (block + 1) * padded]
+        for to_dom in range(dom_size):
+            place, member = to_dom // group_size, to_dom % group_size
+            tile = part[:, place * lanes : (place + 1) * lanes]
+            norm_rows = jnp.concatenate(
+                [tile[class_count:padded], tile[: piece_rows - (padded - class_count)]], axis=0
+            )
+            message = turned(norm_rows, pieces - member)
+            for k in range(pieces):
+                piece = tile[k * piece_rows : (k + 1) * piece_rows]
+                message = jnp.where(lane_group == k, turned(piece, k - member), message)
+            stage[to_dom, block] = message
 
     posts = []
     for index, (to_dom, to_cls) in enumerate(partners):
         copy = pltpu.make_async_remote_copy(
-            src_ref=source(to_dom, to_cls),
-            dst_ref=landing(dom, cls),
+            src_ref=stage.at[to_dom, to_cls],
+            dst_ref=landed.at[cls, dom],
             send_sem=post_send.at[index],
-            recv_sem=post_recv.at[dom, cls],
+            recv_sem=post_recv.at[cls, dom],
             device_id=(to_dom, to_cls),
             device_id_type=MESH,
         )
         copy.start()
         posts.append(copy)
-    own = pltpu.make_async_copy(source(dom, cls), landing(dom, cls), own_sem)
-    own.start()
+    landed[cls, dom] = stage[dom, cls]
     for copy in sends:
         copy.wait_send()
     for copy in posts:
         copy.wait_send()
-    own.wait()
-    for from_dom, from_cls in partners:
+    for from_dom, from_cls in reversed(partners):
         pltpu.make_async_remote_copy(
-            src_ref=source(from_dom, from_cls),
-            dst_ref=landing(from_dom, from_cls),
+            src_ref=stage.at[from_dom, from_cls],
+            dst_ref=landed.at[from_cls, from_dom],
             send_sem=post_send.at[0],
-            recv_sem=post_recv.at[from_dom, from_cls],
+            recv_sem=post_recv.at[from_cls, from_dom],
             device_id=(from_dom, from_cls),
             device_id_type=MESH,
         ).wait_recv()
+
+    for from_cls in range(cls_size):
+        for place in range(dom_size // group_size):
+            low = from_cls * slot_count + place * lanes
+            got = [landed[from_cls, place * group_size + member] for member in range(group_size)]
+            for k in range(group_size):
+                value = turned(got[0], 0 - k)
+                for member in range(1, group_size):
+                    value = jnp.where(
+                        lane_group == member, turned(got[member], member - k), value
+                    )
+                if k < pieces:
+                    out_ref[k * piece_rows : (k + 1) * piece_rows, low : low + lanes] = value
+                else:
+                    log_ref[:, low : low + lanes] = value[0:1]
 
 
 def kernel_shards(images, destinations, group_ids, offsets, inv_noise, ctf_table, references):
@@ -418,61 +512,81 @@
     shift_count = offsets.shape[0]
     class_count, block_columns = references.shape
     slot_count = 2 * local_count
-    padded = -(-(class_count + 1) // 16) * 16
+    lanes = 128
+    piece_rows = class_count // (lanes // (slot_count // dom_size) - 1)
+    padded = class_count + 8
     device_count = dom_size * cls_size
+    table_rows = -(-shift_count // 8) * 8
     vmem = pl.BlockSpec(memory_space=pltpu.VMEM)
-    out = pl.pallas_call(
+    hbm = pl.BlockSpec(memory_space=pltpu.HBM)
+    posteriors, log_norms = pl.pallas_call(
         functools.partial(e_step_kernel, dom_size, cls_size),
-        out_shape=jax.ShapeDtypeStruct((cls_size * slot_count, 128), jnp.float32),
-        in_specs=[pl.BlockSpec(memory_space=pltpu.SMEM)] + [vmem] * 6,
-        out_specs=pl.BlockSpec(memory_space=pl.ANY),
+        out_shape=(
+            jax.ShapeDtypeStruct((class_count, cls_size * slot_count), jnp.float32),
+            jax.ShapeDtypeStruct((1, cls_size * slot_count), jnp.float32),
+        ),
+        in_specs=[pl.BlockSpec(memory_space=pltpu.SMEM), hbm, vmem, vmem, hbm, hbm, hbm],
+        out_specs=(vmem, vmem),
         scratch_shapes=[
+            pltpu.VMEM((local_count, columns), jnp.bfloat16),
+            pltpu.VMEM((1, kept), jnp.float32),
+            pltpu.VMEM((group_count, kept), jnp.float32),
+            pltpu.VMEM((class_count, block_columns), jnp.bfloat16),
             pltpu.VMEM((2, dom_size, cls_size, padded, block_columns // 2), jnp.bfloat16),
             pltpu.VMEM((shift_count * local_count, columns), jnp.bfloat16),
             pltpu.VMEM((3 * group_count, kept), jnp.bfloat16),
-            pltpu.VMEM((3 * group_count, kept), jnp.bfloat16),
-            pltpu.VMEM((2 * shift_count, kept), jnp.float32),
+            pltpu.VMEM((table_rows, kept), jnp.float32),
+            pltpu.VMEM((table_rows, kept), jnp.float32),
             pltpu.VMEM((cls_size * padded, shift_count * local_count), jnp.float32),
-            pltpu.VMEM((cls_size * padded, 3 * group_count), jnp.float32),
-            pltpu.VMEM((cls_size, slot_count, 128), jnp.float32),
+            pltpu.VMEM((2, cls_size, 8, block_columns // 2), jnp.float32),
+            pltpu.VMEM((slot_count, 3 * local_count), jnp.bfloat16),
+            pltpu.VMEM((3 * group_count, local_count), jnp.bfloat16),
+            pltpu.VMEM((dom_size, cls_size, piece_rows, lanes), jnp.float32),
+            pltpu.VMEM((cls_size, dom_size, piece_rows, lanes), jnp.float32),
+            pltpu.SemaphoreType.DMA((4,)),
             pltpu.SemaphoreType.DMA((2 * device_count + dom_size,)),
             pltpu.SemaphoreType.DMA((2, dom_size, cls_size)),
             pltpu.SemaphoreType.DMA((device_count,)),
-            pltpu.SemaphoreType.DMA((dom_size, cls_size)),
-            pltpu.SemaphoreType.DMA,
+            pltpu.SemaphoreType.DMA((cls_size, dom_size)),
         ],
         compiler_params=pltpu.CompilerParams(
-            collective_id=0, has_side_effects=True, vmem_limit_bytes=40 * 1024 * 1024
+            collective_id=0, has_side_effects=True, vmem_limit_bytes=56 * 1024 * 1024
         ),
     )(
-        offsets,
+        offsets.T,
         images,
-        destinations,
+        destinations.T,
         group_ids[None, :],
         inv_noise[None, :],
         ctf_table,
         references,
     )
-    return (out[:, :class_count], out[:, class_count])
-
-
-def fits_kernel(mesh, images, references):
+    return (posteriors.T, log_norms[0])
+
+
+def fits_kernel(mesh, images, ctf_table, references):
     dom_size, cls_size = mesh.shape["dom"], mesh.shape["cls"]
     local_count = images.shape[0] // (dom_size * cls_size)
-    block_columns = references.shape[1] // dom_size
+    capacity = 2 * local_count // dom_size
+    class_count = references.shape[0] // cls_size
+    half_columns = references.shape[1] // dom_size // 2
+    if cls_size != 4 or dom_size % 2 or local_count != 128 or 128 % capacity:
+        return False
+    group_size = 128 // capacity
     return (
-        cls_size == 4
-        and dom_size % 2 == 0
-        and local_count == 128
-        and 2 * local_count // dom_size % 8 == 0
-        and block_columns % 256 == 0
-        and references.shape[0] // cls_size < 128
+        group_size > 1
+        and dom_size % group_size == 0
+        and class_count % (8 * (group_size - 1)) == 0
+        and (class_count + 8) % 16 == 0
+        and half_columns % 128 == 0
+        and 3 * (class_count + 8) < half_columns
+        and ctf_table.shape[0] == 16
     )
 
 
 def solution(mesh):
     def e_step(*arrays):
-        shards = kernel_shards if fits_kernel(mesh, arrays[0], arrays[-1]) else plain_shards
+        shards = kernel_shards if fits_kernel(mesh, arrays[0], arrays[-2], arrays[-1]) else plain_shards
         return mapped(mesh, shards)(*arrays)
 
     return e_step

time: 52.3 us -> 44.3 us (0.85)
  the two profiles are of different devices: /device:TPU:27 before, /device:TPU:0 now
where the time goes in v3:
time: 44.3 us; the launch traced here: 44.2 us
  Pallas kernels  41.2 us (93%)
  local copies, waits for them, and re-layouts  2.29 us (5%)
  between operations  0.65 us (1%)
    pallas_call x1, Pallas kernels, kernel_shards(): pl.pallas_call(functools.partial(e_step_kernel, dom_size, cls_size), out_...  41.2 us
    unnamed x4, local copies, waits for them, and re-layouts  2.29 us

profile of v3, /device:TPU:0, one launch (start us, length us, event | category | flops | bytes accessed | tf_op | source)
XLA Modules:
  0.0 44.2 jit_solution(16403395277304206840)
XLA Ops:
  0.6 41.2 %shard_map.86 = (f32[72,1024]{1,0:T(8,128)}, f32[1,1024]{1,0:T(1,128)}) custom-call(s32[2,3]{1,0:T(2,128)} %bitcast.9, bf16[128,4096]{1,0:T(8,128)(2,1)} %images_hbm.1, s32[1,128]{1,0:T(1,128)} %bitcast.10, s32[1,128]{1,0:T(1,128)} %bitcast.11, f32[1,2048]{1,0:T(1,128)} %bitcast.7, f32[16,2048]{1,0:T(8,128)} %ctf_hbm.1, bf16[72,512]{1,0:T(8,128)(2,1)} %refs_hbm.1), custom_call_target="tpu_custom_call" | custom-call | tf_op jit(solution)/shard_map/pallas_call | solution.py:522
  41.9 0.0 copy-start
  41.9 1.7 %copy.11 = f32[1024,72]{0,1:T(8,128)} copy(f32[1024,72]{0,1:T(8,128)} %bitcast.6) | data formatting | bytes 589824
  43.6 0.0 copy-done
  43.6 0.6 %copy.12 = f32[1024]{0:T(1024)} copy(f32[1024]{0:T(1024)S(1)} %bitcast.8) | data formatting | bytes 8192
Async XLA Ops:
  41.9 1.7 %copy-start = (f32[1,1024]{1,0:T(1,128)S(1)}, f32[1,1024]{1,0:T(1,128)}, u32[]{:S(2)}) copy-start(f32[1,1024]{1,0:T(1,128)} %get-tuple-element.5) | copy-start | bytes 12292

commit v4 on v3

--- a/solution.py
+++ b/solution.py
@@ -191,7 +191,6 @@
     capacity = slot_count // dom_size
     piece_rows, lanes = stage.shape[2:]
     group_size = lanes // capacity
-    pieces = group_size - 1
     dom = lax.axis_index("dom")
     cls = lax.axis_index("cls")
     z, x = dom // 2, dom % 2
@@ -256,12 +255,13 @@
     sends = []
 
     def block_copy(half, block_dom, block_cls, device, index):
-        block = held.at[half, block_dom, block_cls]
+        halves, sem = (slice(None), 0) if half is None else (half, half)
+        block = held.at[halves, block_dom, block_cls]
         return pltpu.make_async_remote_copy(
             src_ref=block,
             dst_ref=block,
             send_sem=send_sem.at[index],
-            recv_sem=recv_sem.at[half, block_dom, block_cls],
+            recv_sem=recv_sem.at[sem, block_dom, block_cls],
             device_id=device,
             device_id_type=MESH,
         )
@@ -274,20 +274,27 @@
     def arrived(half, block_dom, block_cls):
         block_copy(half, block_dom, block_cls, over_core, 0).wait_recv()
 
+    def z_partner(step):
+        other, bit = z, 1
+        while bit < z_size:
+            if step & bit:
+                other = other + bit - 2 * bit * ((z // bit) % 2)
+            bit *= 2
+        return other
+
     over_x = (z * 2 + (1 - x), cls)
     over_y = (dom, (1 - y) * 2 + core)
     over_core = (dom, y * 2 + (1 - core))
-    first = [over_x, over_y]
-    last = [over_y, over_x]
-
-    for half in range(2):
-        send(half, dom, cls, first[half])
-    for step in range(1, z_size):
-        for half in range(2):
-            send(half, dom, cls, (lax.rem(z + step, z_size) * 2 + x, cls))
-    for half in range(2):
-        send(half, dom, cls, last[half])
-        send(half, dom, cls, over_core)
+
+    send(0, dom, cls, over_x)
+    send(1, dom, cls, over_y)
+    for step in range(1, min(2, z_size)):
+        send(None, dom, cls, (z_partner(step) * 2 + x, cls))
+    send(1, dom, cls, over_x)
+    send(0, dom, cls, over_y)
+    for step in range(2, z_size):
+        send(None, dom, cls, (z_partner(step) * 2 + x, cls))
+    send(None, dom, cls, over_core)
 
     table_shape = (cosines.shape[0], kept)
     freq = lax.broadcasted_iota(jnp.int32, table_shape, 1)
@@ -311,7 +318,7 @@
     part_lane = lax.broadcasted_iota(jnp.int32, (local_count, 3 * group_count), 1)
     group_hot = jnp.where(part_lane % group_count == group_col, 1.0, 0.0).astype(jnp.bfloat16)
 
-    chunk = kept // z_size
+    chunk = kept // 4
 
     def shift_chunk(step):
         low = step * chunk
@@ -333,20 +340,6 @@
                 weight * (real_part * sine + imag_part * cosine)
             ).astype(jnp.bfloat16)
 
-    z_order = [0, 1, z_size - 1] + list(range(2, z_size - 1))
-    z_order = z_order[:z_size]
-    loads[3].wait()
-    shift_chunk(0)
-    for count, step in enumerate(z_order[1:]):
-        block = lax.rem(z + step, z_size) * 2 + x
-        for half in range(2):
-            arrived(half, block, cls)
-            send(half, block, cls, first[half])
-        for half in range(2):
-            send(half, block, cls, last[half])
-            send(half, block, cls, over_core)
-        shift_chunk(count + 1)
-
     hot_rows = lax.broadcasted_iota(jnp.int32, group_hot_rows.shape, 0)
     group_hot_rows[...] = jnp.where(hot_rows % group_count == group_row, 1.0, 0.0).astype(
         jnp.bfloat16
@@ -363,20 +356,37 @@
     cross[...] = jnp.zeros_like(cross)
     norms[...] = jnp.zeros_like(norms)
 
-    for step in z_order:
-        block_z = lax.rem(z + step, z_size)
-        for half in range(2):
-            block = (block_z * 2 + (1 - x), cls) if half == 0 else (block_z * 2 + x, over_y[1])
-            arrived(half, *block)
-            send(half, *block, last[half])
-            send(half, *block, over_core)
-
-    sibling = 1 - core
+    def from_z(step):
+        block = z_partner(step) * 2 + x
+        arrived(None, block, cls)
+        send(0, block, cls, over_x)
+        send(1, block, cls, over_y)
+        send(1, block, cls, over_x)
+        send(0, block, cls, over_y)
+        send(None, block, cls, over_core)
+
+    def from_first(step):
+        near, far = z_partner(step) * 2 + x, z_partner(step) * 2 + (1 - x)
+        arrived(0, far, cls)
+        send(0, far, cls, over_y)
+        arrived(1, near, over_y[1])
+        send(1, near, over_y[1], over_x)
+        send(0, far, cls, over_core)
+        send(1, near, over_y[1], over_core)
+
+    def from_last(step):
+        near, far = z_partner(step) * 2 + x, z_partner(step) * 2 + (1 - x)
+        arrived(0, near, over_y[1])
+        send(0, near, over_y[1], over_core)
+        arrived(1, far, cls)
+        send(1, far, cls, over_core)
+        arrived(0, far, over_y[1])
+        arrived(1, far, over_y[1])
+        send(None, far, over_y[1], over_core)
+
+    sibling, far_sibling = over_core[1], (1 - y) * 2 + (1 - core)
 
     def add_block(block_dom):
-        for half in range(2):
-            arrived(half, block_dom, sibling)
-            arrived(half, block_dom, 2 + sibling)
         rows = jnp.concatenate(
             [held[half, block_dom].reshape(cls_size * padded, half_columns) for half in range(2)],
             axis=1,
@@ -389,24 +399,35 @@
             last_rows = held[half, block_dom, :, padded - 16 : padded, :].astype(jnp.float32)
             norms[half] += last_rows[:, 8:16, :]
 
-    waiting = []
-    for near in range(2):
-        for step in z_order:
-            block_z = lax.rem(z + step, z_size)
-            block_dom = block_z * 2 + (x if near == 0 else 1 - x)
-            far_block = block_z * 2 + (1 - x)
-            for half in range(2):
-                if half == 0:
-                    block = (block_dom, over_y[1])
-                else:
-                    block = (far_block, cls if near == 0 else over_y[1])
-                arrived(half, *block)
-                send(half, *block, over_core)
-            waiting.append(block_dom)
-            if len(waiting) > 1:
-                add_block(waiting.pop(0))
-    for item in waiting:
-        add_block(item)
+    def multiply(step):
+        while chunks:
+            shift_chunk(chunks.pop(0))
+        near, far = z_partner(step) * 2 + x, z_partner(step) * 2 + (1 - x)
+        arrived(None, near, sibling)
+        arrived(0, near, far_sibling)
+        arrived(1, near, far_sibling)
+        add_block(near)
+        arrived(0, far, sibling)
+        arrived(1, far, sibling)
+        arrived(None, far, far_sibling)
+        add_block(far)
+
+    chunks = list(range(4))
+    loads[3].wait()
+    shift_chunk(chunks.pop(0))
+    for step in range(z_size + 2):
+        if 0 < step < z_size:
+            from_z(step)
+        if step == 1:
+            shift_chunk(chunks.pop(0))
+        if step >= 2:
+            multiply(step - 2)
+        if step < z_size:
+            from_first(step)
+        if step == 1:
+            shift_chunk(chunks.pop(0))
+        if 0 < step <= z_size:
+            from_last(step - 1)
 
     selected = []
     for block in range(cls_size):
@@ -440,25 +461,42 @@
         NT_DIMS,
         preferred_element_type=jnp.float32,
     )
-    lane_group = lax.broadcasted_iota(jnp.int32, (piece_rows, lanes), 1) // capacity
+    lane_group = lax.broadcasted_iota(jnp.int32, (8, lanes), 1) // capacity
+    whole = class_count // (8 * group_size)
+    left_over = (class_count - whole * 8 * group_size) // group_size
 
     def turned(value, groups):
         amount = groups % group_size * capacity
         return pltpu.roll(value, amount, 1) if amount else value
 
+    def lifted(value, rows):
+        return pltpu.roll(value, rows % 8, 0) if rows % 8 else value
+
+    def side_by_side(values):
+        result = values[0]
+        for k in range(1, group_size):
+            result = jnp.where(lane_group == k, values[k], result)
+        return result
+
+    sub_row = lax.broadcasted_iota(jnp.int32, (8, lanes), 0)
     for block in range(cls_size):
         part = slots[block * padded : (block + 1) * padded]
         for to_dom in range(dom_size):
             place, member = to_dom // group_size, to_dom % group_size
             tile = part[:, place * lanes : (place + 1) * lanes]
-            norm_rows = jnp.concatenate(
-                [tile[class_count:padded], tile[: piece_rows - (padded - class_count)]], axis=0
-            )
-            message = turned(norm_rows, pieces - member)
-            for k in range(pieces):
-                piece = tile[k * piece_rows : (k + 1) * piece_rows]
-                message = jnp.where(lane_group == k, turned(piece, k - member), message)
-            stage[to_dom, block] = message
+            for w in range(whole):
+                values = []
+                for k in range(group_size):
+                    top = 8 * (k * whole + w)
+                    values.append(turned(tile[top : top + 8], k - member))
+                stage[to_dom, block, 8 * w : 8 * w + 8, :] = side_by_side(values)
+            rest = tile[8 * whole * group_size : class_count]
+            values = [
+                turned(lifted(rest, -left_over * k), k - member) for k in range(group_size)
+            ]
+            norm_row = lifted(turned(tile[class_count:padded], -member), left_over)
+            mixed = jnp.where(sub_row < left_over, side_by_side(values), norm_row)
+            stage[to_dom, block, 8 * whole : piece_rows, :] = mixed[: piece_rows - 8 * whole]
 
     posts = []
     for index, (to_dom, to_cls) in enumerate(partners):
@@ -487,20 +525,33 @@
             device_id_type=MESH,
         ).wait_recv()
 
+    def pad_rows(value):
+        empty = jnp.zeros((8 - value.shape[0], lanes), jnp.float32)
+        return jnp.concatenate([value, empty], axis=0)
+
     for from_cls in range(cls_size):
         for place in range(dom_size // group_size):
             low = from_cls * slot_count + place * lanes
             got = [landed[from_cls, place * group_size + member] for member in range(group_size)]
             for k in range(group_size):
-                value = turned(got[0], 0 - k)
-                for member in range(1, group_size):
-                    value = jnp.where(
-                        lane_group == member, turned(got[member], member - k), value
+                for w in range(whole):
+                    top = 8 * (k * whole + w)
+                    out_ref[top : top + 8, low : low + lanes] = side_by_side(
+                        [
+                            turned(value[8 * w : 8 * w + 8], member - k)
+                            for member, value in enumerate(got)
+                        ]
                     )
-                if k < pieces:
-                    out_ref[k * piece_rows : (k + 1) * piece_rows, low : low + lanes] = value
-                else:
-                    log_ref[:, low : low + lanes] = value[0:1]
+                top = 8 * whole * group_size + left_over * k
+                out_ref[top : top + left_over, low : low + lanes] = side_by_side(
+                    [
+                        turned(pad_rows(value[8 * whole :]), member - k)
+                        for member, value in enumerate(got)
+                    ]
+                )[:left_over]
+            log_ref[:, low : low + lanes] = side_by_side(
+                [turned(pad_rows(value[8 * whole :]), member) for member, value in enumerate(got)]
+            )[left_over : left_over + 1]
 
 
 def kernel_shards(images, destinations, group_ids, offsets, inv_noise, ctf_table, references):
@@ -513,7 +564,7 @@
     class_count, block_columns = references.shape
     slot_count = 2 * local_count
     lanes = 128
-    piece_rows = class_count // (lanes // (slot_count // dom_size) - 1)
+    piece_rows = class_count // (lanes // (slot_count // dom_size)) + 1
     padded = class_count + 8
     device_count = dom_size * cls_size
     table_rows = -(-shift_count // 8) * 8
@@ -550,7 +601,7 @@
             pltpu.SemaphoreType.DMA((cls_size, dom_size)),
         ],
         compiler_params=pltpu.CompilerParams(
-            collective_id=0, has_side_effects=True, vmem_limit_bytes=56 * 1024 * 1024
+            collective_id=0, has_side_effects=True, vmem_limit_bytes=24 * 1024 * 1024
         ),
     )(
         offsets.T,
@@ -576,7 +627,11 @@
     return (
         group_size > 1
         and dom_size % group_size == 0
-        and class_count % (8 * (group_size - 1)) == 0
+        and class_count % 8 == 0
+        and class_count % (8 * group_size) == 8
+        and 8 // group_size * group_size == 8
+        and 8 // group_size < 8
+        and dom_size & (dom_size - 1) == 0
         and (class_count + 8) % 16 == 0
         and half_columns % 128 == 0
         and 3 * (class_count + 8) < half_columns

time: 44.3 us -> 44.9 us (1.014)
  local copies, waits for them, and re-layouts: 2.29 us -> 5.69 us
  Pallas kernels: 41.2 us -> 38.2 us
    unnamed x4 -> x16, local copies, waits for them, and re-layouts: 2.29 us -> 5.69 us
    pallas_call x1, Pallas kernels: 41.2 us -> 38.2 us  [kernel_shards(): pl.pallas_call(functools.partial(e_step_kernel, dom_size, cls_size), out_...]
where the time goes in v4:
time: 44.9 us; the launch traced here: 44.6 us
  Pallas kernels  38.2 us (85%)
  local copies, waits for them, and re-layouts  5.69 us (13%)
  between operations  0.67 us (1%)
    pallas_call x1, Pallas kernels, kernel_shards(): pl.pallas_call(functools.partial(e_step_kernel, dom_size, cls_size), out_...  38.2 us
    unnamed x16, local copies, waits for them, and re-layouts  5.69 us

profile of v4, /device:TPU:0, one launch (start us, length us, event | category | flops | bytes accessed | tf_op | source)
XLA Modules:
  0.0 44.6 jit_solution(17063114880308134639)
XLA Ops:
  0.6 0.0 copy-start.6
  0.6 0.0 copy-start.4
  0.7 0.0 copy-start.5
  0.7 0.6 %copy-done.6 = s32[128]{0:T(128)S(1)} copy-done((s32[128]{0:T(128)S(1)}, s32[128]{0:T(128)}, u32[]{:S(2)}) %copy-start.6) | copy-done | bytes 536
  1.3 0.0 copy-done.4
  1.3 0.0 copy-done.5
  1.3 0.0 copy-start
  1.3 1.2 %copy-done = bf16[128,4096]{1,0:T(8,128)(2,1)S(1)} copy-done((bf16[128,4096]{1,0:T(8,128)(2,1)S(1)}, bf16[128,4096]{1,0:T(8,128)(2,1)}, u32[]{:S(2)}) %copy-start) | copy-done | bytes 1048600
  2.6 0.0 copy-start.1
  2.6 0.9 %copy-done.1 = f32[16,2048]{1,0:T(8,128)S(1)} copy-done((f32[16,2048]{1,0:T(8,128)S(1)}, f32[16,2048]{1,0:T(8,128)}, u32[]{:S(2)}) %copy-start.1) | copy-done | bytes 131096
  3.5 0.0 copy-start.2
  3.5 0.9 %copy-done.2 = bf16[72,512]{1,0:T(8,128)(2,1)S(1)} copy-done((bf16[72,512]{1,0:T(8,128)(2,1)S(1)}, bf16[72,512]{1,0:T(8,128)(2,1)}, u32[]{:S(2)}) %copy-start.2) | copy-done | bytes 73752
  4.3 0.0 copy-start.3
  4.3 0.7 %copy-done.3 = f32[2048]{0:T(1024)S(1)} copy-done((f32[2048]{0:T(1024)S(1)}, f32[2048]{0:T(1024)}, u32[]{:S(2)}) %copy-start.3) | copy-done | bytes 8216
  5.0 38.2 %shard_map.86 = (f32[72,1024]{1,0:T(8,128)S(1)}, f32[1,1024]{1,0:T(1,128)S(1)}) custom-call(s32[2,3]{1,0:T(2,128)S(1)} %bitcast.9, bf16[128,4096]{1,0:T(8,128)(2,1)S(1)} %copy-done, s32[1,128]{1,0:T(1,128)S(1)} %bitcast.10, s32[1,128]{1,0:T(1,128)S(1)} %bitcast.11, f32[1,2048]{1,0:T(1,128)S(1)} %bitcast.7, f32[16,2048]{1,0:T(8,128)S(1)} %copy-done.1, ...), custom_call_target="tpu_custom_call" | custom-call | tf_op jit(solution)/shard_map/pallas_call | solution.py:573
  43.3 0.7 %copy.11 = f32[1024,72]{0,1:T(8,128)} copy(f32[1024,72]{0,1:T(8,128)S(1)} %bitcast.6) | data formatting | bytes 589824
  44.0 0.6 %copy.12 = f32[1024]{0:T(1024)} copy(f32[1024]{0:T(1024)S(1)} %bitcast.8) | data formatting | bytes 8192
Async XLA Ops:
  0.6 0.7 %copy-start.6 = (s32[128]{0:T(128)S(1)}, s32[128]{0:T(128)}, u32[]{:S(2)}) copy-start(s32[128]{0:T(128)} %param.9) | copy-start | bytes 1540
  0.6 0.7 %copy-start.4 = (s32[3,2]{0,1:T(2,128)S(1)}, s32[3,2]{0,1:T(2,128)}, u32[]{:S(2)}) copy-start(s32[3,2]{0,1:T(2,128)} %param.10) | copy-start | bytes 76
  0.7 0.7 %copy-start.5 = (s32[128,1]{0,1:T(1,128)S(1)}, s32[128,1]{0,1:T(1,128)}, u32[]{:S(2)}) copy-start(s32[128,1]{0,1:T(1,128)} %param.8) | copy-start | bytes 1540
  1.3 1.2 %copy-start = (bf16[128,4096]{1,0:T(8,128)(2,1)S(1)}, bf16[128,4096]{1,0:T(8,128)(2,1)}, u32[]{:S(2)}) copy-start(bf16[128,4096]{1,0:T(8,128)(2,1)} %images_hbm.1) | copy-start | bytes 3145732
  2.6 0.9 %copy-start.1 = (f32[16,2048]{1,0:T(8,128)S(1)}, f32[16,2048]{1,0:T(8,128)}, u32[]{:S(2)}) copy-start(f32[16,2048]{1,0:T(8,128)} %ctf_hbm.1) | copy-start | bytes 393220
  3.5 0.9 %copy-start.2 = (bf16[72,512]{1,0:T(8,128)(2,1)S(1)}, bf16[72,512]{1,0:T(8,128)(2,1)}, u32[]{:S(2)}) copy-start(bf16[72,512]{1,0:T(8,128)(2,1)} %refs_hbm.1) | copy-start | bytes 221188
  4.3 0.7 %copy-start.3 = (f32[2048]{0:T(1024)S(1)}, f32[2048]{0:T(1024)}, u32[]{:S(2)}) copy-start(f32[2048]{0:T(1024)} %param.11) | copy-start | bytes 24580

commit v5 on v4

--- a/solution.py
+++ b/solution.py
@@ -156,8 +156,7 @@
     inv_noise_hbm,
     ctf_hbm,
     refs_hbm,
-    out_ref,
-    log_ref,
+    landed,
     images_ref,
     inv_noise_ref,
     ctf_ref,
@@ -172,12 +171,12 @@
     slot_hot,
     group_hot_rows,
     stage,
-    landed,
     load_sem,
     send_sem,
     recv_sem,
     post_send,
     post_recv,
+    own_sem,
 ):
     z_size = dom_size // 2
     class_count, block_columns = refs_ref.shape
@@ -368,9 +367,11 @@
     def from_first(step):
         near, far = z_partner(step) * 2 + x, z_partner(step) * 2 + (1 - x)
         arrived(0, far, cls)
-        send(0, far, cls, over_y)
+        if step % 2 == 0:
+            send(0, far, cls, over_y)
         arrived(1, near, over_y[1])
-        send(1, near, over_y[1], over_x)
+        if step % 2 == 0:
+            send(1, near, over_y[1], over_x)
         send(0, far, cls, over_core)
         send(1, near, over_y[1], over_core)
 
@@ -380,8 +381,13 @@
         send(0, near, over_y[1], over_core)
         arrived(1, far, cls)
         send(1, far, cls, over_core)
-        arrived(0, far, over_y[1])
-        arrived(1, far, over_y[1])
+        if step % 2 == 0:
+            arrived(0, far, over_y[1])
+            arrived(1, far, over_y[1])
+            if z_size > 1:
+                send(None, far, over_y[1], (z_partner(1) * 2 + x, cls))
+        else:
+            arrived(None, far, over_y[1])
         send(None, far, over_y[1], over_core)
 
     sibling, far_sibling = over_core[1], (1 - y) * 2 + (1 - core)
@@ -510,11 +516,13 @@
         )
         copy.start()
         posts.append(copy)
-    landed[cls, dom] = stage[dom, cls]
+    own = pltpu.make_async_copy(stage.at[dom, cls], landed.at[cls, dom], own_sem)
+    own.start()
     for copy in sends:
         copy.wait_send()
     for copy in posts:
         copy.wait_send()
+    own.wait()
     for from_dom, from_cls in reversed(partners):
         pltpu.make_async_remote_copy(
             src_ref=stage.at[from_dom, from_cls],
@@ -525,33 +533,51 @@
             device_id_type=MESH,
         ).wait_recv()
 
+
+def unpack_kernel(capacity, landed, out_ref, log_ref):
+    dom_size, piece_rows, lanes = landed.shape[1:]
+    class_count = out_ref.shape[0]
+    group_size = lanes // capacity
+    lane_group = lax.broadcasted_iota(jnp.int32, (8, lanes), 1) // capacity
+    whole = class_count // (8 * group_size)
+    left_over = (class_count - whole * 8 * group_size) // group_size
+
+    def turned(value, groups):
+        amount = groups % group_size * capacity
+        return pltpu.roll(value, amount, 1) if amount else value
+
+    def side_by_side(values):
+        result = values[0]
+        for k in range(1, group_size):
+            result = jnp.where(lane_group == k, values[k], result)
+        return result
+
     def pad_rows(value):
         empty = jnp.zeros((8 - value.shape[0], lanes), jnp.float32)
         return jnp.concatenate([value, empty], axis=0)
 
-    for from_cls in range(cls_size):
-        for place in range(dom_size // group_size):
-            low = from_cls * slot_count + place * lanes
-            got = [landed[from_cls, place * group_size + member] for member in range(group_size)]
-            for k in range(group_size):
-                for w in range(whole):
-                    top = 8 * (k * whole + w)
-                    out_ref[top : top + 8, low : low + lanes] = side_by_side(
-                        [
-                            turned(value[8 * w : 8 * w + 8], member - k)
-                            for member, value in enumerate(got)
-                        ]
-                    )
-                top = 8 * whole * group_size + left_over * k
-                out_ref[top : top + left_over, low : low + lanes] = side_by_side(
+    for place in range(dom_size // group_size):
+        low = place * lanes
+        got = [landed[0, place * group_size + member] for member in range(group_size)]
+        for k in range(group_size):
+            for w in range(whole):
+                top = 8 * (k * whole + w)
+                out_ref[top : top + 8, low : low + lanes] = side_by_side(
                     [
-                        turned(pad_rows(value[8 * whole :]), member - k)
+                        turned(value[8 * w : 8 * w + 8], member - k)
                         for member, value in enumerate(got)
                     ]
-                )[:left_over]
-            log_ref[:, low : low + lanes] = side_by_side(
-                [turned(pad_rows(value[8 * whole :]), member) for member, value in enumerate(got)]
-            )[left_over : left_over + 1]
+                )
+            top = 8 * whole * group_size + left_over * k
+            out_ref[top : top + left_over, low : low + lanes] = side_by_side(
+                [
+                    turned(pad_rows(value[8 * whole :]), member - k)
+                    for member, value in enumerate(got)
+                ]
+            )[:left_over]
+        log_ref[:, low : low + lanes] = side_by_side(
+            [turned(pad_rows(value[8 * whole :]), member) for member, value in enumerate(got)]
+        )[left_over : left_over + 1]
 
 
 def kernel_shards(images, destinations, group_ids, offsets, inv_noise, ctf_table, references):
@@ -570,14 +596,11 @@
     table_rows = -(-shift_count // 8) * 8
     vmem = pl.BlockSpec(memory_space=pltpu.VMEM)
     hbm = pl.BlockSpec(memory_space=pltpu.HBM)
-    posteriors, log_norms = pl.pallas_call(
+    packed = pl.pallas_call(
         functools.partial(e_step_kernel, dom_size, cls_size),
-        out_shape=(
-            jax.ShapeDtypeStruct((class_count, cls_size * slot_count), jnp.float32),
-            jax.ShapeDtypeStruct((1, cls_size * slot_count), jnp.float32),
-        ),
+        out_shape=jax.ShapeDtypeStruct((cls_size, dom_size, piece_rows, lanes), jnp.float32),
         in_specs=[pl.BlockSpec(memory_space=pltpu.SMEM), hbm, vmem, vmem, hbm, hbm, hbm],
-        out_specs=(vmem, vmem),
+        out_specs=hbm,
         scratch_shapes=[
             pltpu.VMEM((local_count, columns), jnp.bfloat16),
             pltpu.VMEM((1, kept), jnp.float32),
@@ -593,15 +616,15 @@
             pltpu.VMEM((slot_count, 3 * local_count), jnp.bfloat16),
             pltpu.VMEM((3 * group_count, local_count), jnp.bfloat16),
             pltpu.VMEM((dom_size, cls_size, piece_rows, lanes), jnp.float32),
-            pltpu.VMEM((cls_size, dom_size, piece_rows, lanes), jnp.float32),
             pltpu.SemaphoreType.DMA((4,)),
             pltpu.SemaphoreType.DMA((2 * device_count + dom_size,)),
             pltpu.SemaphoreType.DMA((2, dom_size, cls_size)),
             pltpu.SemaphoreType.DMA((device_count,)),
             pltpu.SemaphoreType.DMA((cls_size, dom_size)),
+            pltpu.SemaphoreType.DMA,
         ],
         compiler_params=pltpu.CompilerParams(
-            collective_id=0, has_side_effects=True, vmem_limit_bytes=24 * 1024 * 1024
+            collective_id=0, has_side_effects=True, vmem_limit_bytes=56 * 1024 * 1024
         ),
     )(
         offsets.T,
@@ -612,6 +635,19 @@
         ctf_table,
         references,
     )
+    posteriors, log_norms = pl.pallas_call(
+        functools.partial(unpack_kernel, slot_count // dom_size),
+        out_shape=(
+            jax.ShapeDtypeStruct((class_count, cls_size * slot_count), jnp.float32),
+            jax.ShapeDtypeStruct((1, cls_size * slot_count), jnp.float32),
+        ),
+        grid=(cls_size,),
+        in_specs=[pl.BlockSpec((1, dom_size, piece_rows, lanes), lambda c: (c, 0, 0, 0))],
+        out_specs=(
+            pl.BlockSpec((class_count, slot_count), lambda c: (0, c)),
+            pl.BlockSpec((1, slot_count), lambda c: (0, c)),
+        ),
+    )(packed)
     return (posteriors.T, log_norms[0])
 
 

time: 44.9 us -> 42.4 us (0.944)
  local copies, waits for them, and re-layouts: 5.69 us -> 0 us
  Pallas kernels: 38.2 us -> 41.5 us
    unnamed x16 -> x0, local copies, waits for them, and re-layouts: 5.69 us -> none
    pallas_call x0 -> x1, Pallas kernels: none -> 3.36 us  [kernel_shards(): pl.pallas_call(functools.partial(unpack_kernel, slot_count // dom_size),...]
where the time goes in v5:
time: 42.4 us; the launch traced here: 42.2 us
  Pallas kernels  41.5 us (98%)
  between operations  0.64 us (2%)
    pallas_call x1, Pallas kernels, kernel_shards(): pl.pallas_call(functools.partial(e_step_kernel, dom_size, cls_size), out_...  38.2 us
    pallas_call x1, Pallas kernels, kernel_shards(): pl.pallas_call(functools.partial(unpack_kernel, slot_count // dom_size),...  3.36 us

profile of v5, /device:TPU:0, one launch (start us, length us, event | category | flops | bytes accessed | tf_op | source)
XLA Modules:
  0.0 42.2 jit_solution(4409501178295828076)
XLA Ops:
  0.6 38.2 %shard_map.86.landed = f32[4,8,19,128]{3,2,1,0:T(8,128)} custom-call(s32[2,3]{1,0:T(2,128)} %bitcast.7, bf16[128,4096]{1,0:T(8,128)(2,1)} %images_hbm.1, s32[1,128]{1,0:T(1,128)} %bitcast.8, s32[1,128]{1,0:T(1,128)} %bitcast.9, f32[1,2048]{1,0:T(1,128)} %bitcast.6, f32[16,2048]{1,0:T(8,128)} %ctf_hbm.1, bf16[72,512]{1,0:T(8,128)(2,1)} %refs_hbm.1), custom_call_target="tpu_custom_call" | custom-call | tf_op jit(solution)/shard_map/pallas_call | solution.py:599
  38.8 3.4 %shard_map.87 = (f32[72,1024]{1,0:T(8,128)}, f32[1,1024]{1,0:T(1,128)}) custom-call(f32[4,8,19,128]{3,2,1,0:T(8,128)} %shard_map.86.landed), custom_call_target="tpu_custom_call" | custom-call | tf_op jit(solution)/shard_map/pallas_call | solution.py:638

commit v6 on v5

--- a/solution.py
+++ b/solution.py
@@ -170,6 +170,7 @@
     norms,
     slot_hot,
     group_hot_rows,
+    slots_ref,
     stage,
     load_sem,
     send_sem,
@@ -210,12 +211,15 @@
         load.start()
     barrier = pltpu.get_barrier_semaphore()
     partners = [
-        (lax.rem(dom + i, dom_size), lax.rem(cls + j, cls_size))
-        for i in sorted(range(dom_size), key=lambda i: (abs(i - dom_size // 2), i))
+        [
+            (lax.rem(dom + i, dom_size), lax.rem(cls + j, cls_size))
+            for i in sorted(range(dom_size), key=lambda i: (abs(i - dom_size // 2), i))
+            if i or j
+        ]
         for j in range(cls_size)
-        if i or j
     ]
-    for partner in partners:
+    every_partner = sum(partners, [])
+    for partner in every_partner:
         pl.semaphore_signal(barrier, inc=1, device_id=partner, device_id_type=MESH)
 
     for load in loads[:3]:
@@ -249,7 +253,7 @@
         extra = padded - class_count
         block = jnp.concatenate([rows, tail[half * extra : (half + 1) * extra]], axis=0)
         held[half, dom, cls] = block.astype(jnp.bfloat16)
-    pl.semaphore_wait(barrier, len(partners))
+    pl.semaphore_wait(barrier, len(every_partner))
 
     sends = []
 
@@ -405,14 +409,17 @@
             last_rows = held[half, block_dom, :, padded - 16 : padded, :].astype(jnp.float32)
             norms[half] += last_rows[:, 8:16, :]
 
-    def multiply(step):
+    def multiply_near(step):
         while chunks:
             shift_chunk(chunks.pop(0))
-        near, far = z_partner(step) * 2 + x, z_partner(step) * 2 + (1 - x)
+        near = z_partner(step) * 2 + x
         arrived(None, near, sibling)
         arrived(0, near, far_sibling)
         arrived(1, near, far_sibling)
         add_block(near)
+
+    def multiply_far(step):
+        far = z_partner(step) * 2 + (1 - x)
         arrived(0, far, sibling)
         arrived(1, far, sibling)
         arrived(None, far, far_sibling)
@@ -427,9 +434,11 @@
         if step == 1:
             shift_chunk(chunks.pop(0))
         if step >= 2:
-            multiply(step - 2)
+            multiply_near(step - 2)
         if step < z_size:
             from_first(step)
+        if step >= 2:
+            multiply_far(step - 2)
         if step == 1:
             shift_chunk(chunks.pop(0))
         if 0 < step <= z_size:
@@ -461,7 +470,7 @@
     log_norm = peak + jnp.log(total)
     table = jnp.where(row == class_count, log_norm, weights / total)
 
-    slots = lax.dot_general(
+    slots_ref[...] = lax.dot_general(
         jnp.concatenate(three_parts(table), axis=1),
         slot_hot[...],
         NT_DIMS,
@@ -485,8 +494,10 @@
         return result
 
     sub_row = lax.broadcasted_iota(jnp.int32, (8, lanes), 0)
-    for block in range(cls_size):
-        part = slots[block * padded : (block + 1) * padded]
+    posts = []
+    for turn in range(cls_size):
+        block = lax.rem(cls + turn, cls_size)
+        part = slots_ref[pl.ds(pl.multiple_of(block * padded, 16), padded), :]
         for to_dom in range(dom_size):
             place, member = to_dom // group_size, to_dom % group_size
             tile = part[:, place * lanes : (place + 1) * lanes]
@@ -503,19 +514,17 @@
             norm_row = lifted(turned(tile[class_count:padded], -member), left_over)
             mixed = jnp.where(sub_row < left_over, side_by_side(values), norm_row)
             stage[to_dom, block, 8 * whole : piece_rows, :] = mixed[: piece_rows - 8 * whole]
-
-    posts = []
-    for index, (to_dom, to_cls) in enumerate(partners):
-        copy = pltpu.make_async_remote_copy(
-            src_ref=stage.at[to_dom, to_cls],
-            dst_ref=landed.at[cls, dom],
-            send_sem=post_send.at[index],
-            recv_sem=post_recv.at[cls, dom],
-            device_id=(to_dom, to_cls),
-            device_id_type=MESH,
-        )
-        copy.start()
-        posts.append(copy)
+        for to_dom, to_cls in partners[turn]:
+            copy = pltpu.make_async_remote_copy(
+                src_ref=stage.at[to_dom, to_cls],
+                dst_ref=landed.at[cls, dom],
+                send_sem=post_send.at[len(posts)],
+                recv_sem=post_recv.at[cls, dom],
+                device_id=(to_dom, to_cls),
+                device_id_type=MESH,
+            )
+            copy.start()
+            posts.append(copy)
     own = pltpu.make_async_copy(stage.at[dom, cls], landed.at[cls, dom], own_sem)
     own.start()
     for copy in sends:
@@ -523,7 +532,7 @@
     for copy in posts:
         copy.wait_send()
     own.wait()
-    for from_dom, from_cls in reversed(partners):
+    for from_dom, from_cls in every_partner:
         pltpu.make_async_remote_copy(
             src_ref=stage.at[from_dom, from_cls],
             dst_ref=landed.at[from_cls, from_dom],
@@ -534,8 +543,10 @@
         ).wait_recv()
 
 
-def unpack_kernel(capacity, landed, out_ref, log_ref):
-    dom_size, piece_rows, lanes = landed.shape[1:]
+def unpack_kernel(
+    capacity, landed_hbm, out_hbm, log_hbm, landed, out_ref, log_ref, in_sem, out_sem, log_sem
+):
+    cls_size, dom_size, piece_rows, lanes = landed.shape
     class_count = out_ref.shape[0]
     group_size = lanes // capacity
     lane_group = lax.broadcasted_iota(jnp.int32, (8, lanes), 1) // capacity
@@ -556,28 +567,48 @@
         empty = jnp.zeros((8 - value.shape[0], lanes), jnp.float32)
         return jnp.concatenate([value, empty], axis=0)
 
-    for place in range(dom_size // group_size):
-        low = place * lanes
-        got = [landed[0, place * group_size + member] for member in range(group_size)]
-        for k in range(group_size):
-            for w in range(whole):
-                top = 8 * (k * whole + w)
-                out_ref[top : top + 8, low : low + lanes] = side_by_side(
+    slot_count = dom_size * capacity
+    loads = [
+        pltpu.make_async_copy(landed_hbm.at[block], landed.at[block], in_sem.at[block])
+        for block in range(cls_size)
+    ]
+    for load in loads:
+        load.start()
+    stores = []
+    for block in range(cls_size):
+        loads[block].wait()
+        for place in range(dom_size // group_size):
+            low = block * slot_count + place * lanes
+            got = [landed[block, place * group_size + member] for member in range(group_size)]
+            for k in range(group_size):
+                for w in range(whole):
+                    top = 8 * (k * whole + w)
+                    out_ref[top : top + 8, low : low + lanes] = side_by_side(
+                        [
+                            turned(value[8 * w : 8 * w + 8], member - k)
+                            for member, value in enumerate(got)
+                        ]
+                    )
+                top = 8 * whole * group_size + left_over * k
+                out_ref[top : top + left_over, low : low + lanes] = side_by_side(
                     [
-                        turned(value[8 * w : 8 * w + 8], member - k)
+                        turned(pad_rows(value[8 * whole :]), member - k)
                         for member, value in enumerate(got)
                     ]
-                )
-            top = 8 * whole * group_size + left_over * k
-            out_ref[top : top + left_over, low : low + lanes] = side_by_side(
-                [
-                    turned(pad_rows(value[8 * whole :]), member - k)
-                    for member, value in enumerate(got)
-                ]
-            )[:left_over]
-        log_ref[:, low : low + lanes] = side_by_side(
-            [turned(pad_rows(value[8 * whole :]), member) for member, value in enumerate(got)]
-        )[left_over : left_over + 1]
+                )[:left_over]
+            log_ref[:, low : low + lanes] = side_by_side(
+                [turned(pad_rows(value[8 * whole :]), member) for member, value in enumerate(got)]
+            )[left_over : left_over + 1]
+        columns = slice(block * slot_count, (block + 1) * slot_count)
+        store = pltpu.make_async_copy(
+            out_ref.at[:, columns], out_hbm.at[:, columns], out_sem.at[block]
+        )
+        store.start()
+        stores.append(store)
+    store = pltpu.make_async_copy(log_ref, log_hbm, log_sem)
+    store.start()
+    for store in stores + [store]:
+        store.wait()
 
 
 def kernel_shards(images, destinations, group_ids, offsets, inv_noise, ctf_table, references):
@@ -615,6 +646,7 @@
             pltpu.VMEM((2, cls_size, 8, block_columns // 2), jnp.float32),
             pltpu.VMEM((slot_count, 3 * local_count), jnp.bfloat16),
             pltpu.VMEM((3 * group_count, local_count), jnp.bfloat16),
+            pltpu.VMEM((cls_size * padded, slot_count), jnp.float32),
             pltpu.VMEM((dom_size, cls_size, piece_rows, lanes), jnp.float32),
             pltpu.SemaphoreType.DMA((4,)),
             pltpu.SemaphoreType.DMA((2 * device_count + dom_size,)),
@@ -641,12 +673,17 @@
             jax.ShapeDtypeStruct((class_count, cls_size * slot_count), jnp.float32),
             jax.ShapeDtypeStruct((1, cls_size * slot_count), jnp.float32),
         ),
-        grid=(cls_size,),
-        in_specs=[pl.BlockSpec((1, dom_size, piece_rows, lanes), lambda c: (c, 0, 0, 0))],
-        out_specs=(
-            pl.BlockSpec((class_count, slot_count), lambda c: (0, c)),
-            pl.BlockSpec((1, slot_count), lambda c: (0, c)),
-        ),
+        in_specs=[hbm],
+        out_specs=(hbm, hbm),
+        scratch_shapes=[
+            pltpu.VMEM((cls_size, dom_size, piece_rows, lanes), jnp.float32),
+            pltpu.VMEM((class_count, cls_size * slot_count), jnp.float32),
+            pltpu.VMEM((1, cls_size * slot_count), jnp.float32),
+            pltpu.SemaphoreType.DMA((cls_size,)),
+            pltpu.SemaphoreType.DMA((cls_size,)),
+            pltpu.SemaphoreType.DMA,
+        ],
+        compiler_params=pltpu.CompilerParams(vmem_limit_bytes=56 * 1024 * 1024),
     )(packed)
     return (posteriors.T, log_norms[0])
 

time: 42.4 us -> 42 us (level)
    pallas_call x1, Pallas kernels: 3.36 us -> 2.17 us  [kernel_shards(): pl.pallas_call(functools.partial(unpack_kernel, slot_count // dom_size),...]
    pallas_call x1, Pallas kernels: 38.2 us -> 38.9 us  [kernel_shards(): pl.pallas_call(functools.partial(e_step_kernel, dom_size, cls_size), out_...]
where the time goes in v6:
time: 42 us; the launch traced here: 41.8 us
  Pallas kernels  41.1 us (98%)
  between operations  0.64 us (2%)
    pallas_call x1, Pallas kernels, kernel_shards(): pl.pallas_call(functools.partial(e_step_kernel, dom_size, cls_size), out_...  38.9 us
    pallas_call x1, Pallas kernels, kernel_shards(): pl.pallas_call(functools.partial(unpack_kernel, slot_count // dom_size),...  2.17 us

profile of v6, /device:TPU:0, one launch (start us, length us, event | category | flops | bytes accessed | tf_op | source)
XLA Modules:
  0.0 41.8 jit_solution(5261748136769879009)
XLA Ops:
  0.6 38.9 %shard_map.86.landed_hbm = f32[4,8,19,128]{3,2,1,0:T(8,128)} custom-call(s32[2,3]{1,0:T(2,128)} %bitcast.7, bf16[128,4096]{1,0:T(8,128)(2,1)} %images_hbm.1, s32[1,128]{1,0:T(1,128)} %bitcast.8, s32[1,128]{1,0:T(1,128)} %bitcast.9, f32[1,2048]{1,0:T(1,128)} %bitcast.6, f32[16,2048]{1,0:T(8,128)} %ctf_hbm.1, bf16[72,512]{1,0:T(8,128)(2,1)} %refs_hbm.1), custom_call_target="tpu_custom_call" | custom-call | tf_op jit(solution)/shard_map/pallas_call | solution.py:630
  39.6 2.2 %shard_map.87 = (f32[72,1024]{1,0:T(8,128)}, f32[1,1024]{1,0:T(1,128)}) custom-call(f32[4,8,19,128]{3,2,1,0:T(8,128)} %shard_map.86.landed_hbm), custom_call_target="tpu_custom_call" | custom-call | tf_op jit(solution)/shard_map/pallas_call | solution.py:670

commit v7 on v6

--- a/solution.py
+++ b/solution.py
@@ -219,7 +219,21 @@
         for j in range(cls_size)
     ]
     every_partner = sum(partners, [])
-    for partner in every_partner:
+    def z_partner(step):
+        other, bit = z, 1
+        while bit < z_size:
+            if step & bit:
+                other = other + bit - 2 * bit * ((z // bit) % 2)
+            bit *= 2
+        return other
+
+    order = list(range(0, z_size, 2)) + list(range(1, z_size, 2))
+    over_x = (z * 2 + (1 - x), cls)
+    over_y = (dom, (1 - y) * 2 + core)
+    over_core = (dom, y * 2 + (1 - core))
+    neighbours = [over_x, over_y, over_core]
+    neighbours += [(z_partner(step) * 2 + x, cls) for step in order[1:]]
+    for partner in neighbours:
         pl.semaphore_signal(barrier, inc=1, device_id=partner, device_id_type=MESH)
 
     for load in loads[:3]:
@@ -253,7 +267,7 @@
         extra = padded - class_count
         block = jnp.concatenate([rows, tail[half * extra : (half + 1) * extra]], axis=0)
         held[half, dom, cls] = block.astype(jnp.bfloat16)
-    pl.semaphore_wait(barrier, len(every_partner))
+    pl.semaphore_wait(barrier, len(neighbours))
 
     sends = []
 
@@ -277,25 +291,13 @@
     def arrived(half, block_dom, block_cls):
         block_copy(half, block_dom, block_cls, over_core, 0).wait_recv()
 
-    def z_partner(step):
-        other, bit = z, 1
-        while bit < z_size:
-            if step & bit:
-                other = other + bit - 2 * bit * ((z // bit) % 2)
-            bit *= 2
-        return other
-
-    over_x = (z * 2 + (1 - x), cls)
-    over_y = (dom, (1 - y) * 2 + core)
-    over_core = (dom, y * 2 + (1 - core))
-
     send(0, dom, cls, over_x)
     send(1, dom, cls, over_y)
-    for step in range(1, min(2, z_size)):
+    for step in order[1:2]:
         send(None, dom, cls, (z_partner(step) * 2 + x, cls))
     send(1, dom, cls, over_x)
     send(0, dom, cls, over_y)
-    for step in range(2, z_size):
+    for step in order[2:]:
         send(None, dom, cls, (z_partner(step) * 2 + x, cls))
     send(None, dom, cls, over_core)
 
@@ -428,21 +430,21 @@
     chunks = list(range(4))
     loads[3].wait()
     shift_chunk(chunks.pop(0))
-    for step in range(z_size + 2):
-        if 0 < step < z_size:
-            from_z(step)
-        if step == 1:
+    for turn in range(z_size + 2):
+        if 0 < turn < z_size:
+            from_z(order[turn])
+        if turn == 1:
             shift_chunk(chunks.pop(0))
-        if step >= 2:
-            multiply_near(step - 2)
-        if step < z_size:
-            from_first(step)
-        if step >= 2:
-            multiply_far(step - 2)
-        if step == 1:
+        if turn >= 2:
+            multiply_near(order[turn - 2])
+        if turn < z_size:
+            from_first(order[turn])
+        if turn >= 2:
+            multiply_far(order[turn - 2])
+        if turn == 1:
             shift_chunk(chunks.pop(0))
-        if 0 < step <= z_size:
-            from_last(step - 1)
+        if 0 < turn <= z_size:
+            from_last(order[turn - 1])
 
     selected = []
     for block in range(cls_size):

time: 42 us -> 39.6 us (0.943)
  Pallas kernels: 41.1 us -> 38.4 us
    pallas_call x1, Pallas kernels: 38.9 us -> 36.2 us  [kernel_shards(): pl.pallas_call(functools.partial(e_step_kernel, dom_size, cls_size), out_...]
where the time goes in v7:
time: 39.6 us; the launch traced here: 39 us
  Pallas kernels  38.4 us (97%)
  between operations  0.64 us (2%)
    pallas_call x1, Pallas kernels, kernel_shards(): pl.pallas_call(functools.partial(e_step_kernel, dom_size, cls_size), out_...  36.2 us
    pallas_call x1, Pallas kernels, kernel_shards(): pl.pallas_call(functools.partial(unpack_kernel, slot_count // dom_size),...  2.17 us

profile of v7, /device:TPU:0, one launch (start us, length us, event | category | flops | bytes accessed | tf_op | source)
XLA Modules:
  0.0 39.0 jit_solution(15103286287429346952)
XLA Ops:
  0.6 36.2 %shard_map.86.landed_hbm = f32[4,8,19,128]{3,2,1,0:T(8,128)} custom-call(s32[2,3]{1,0:T(2,128)} %bitcast.7, bf16[128,4096]{1,0:T(8,128)(2,1)} %images_hbm.1, s32[1,128]{1,0:T(1,128)} %bitcast.8, s32[1,128]{1,0:T(1,128)} %bitcast.9, f32[1,2048]{1,0:T(1,128)} %bitcast.6, f32[16,2048]{1,0:T(8,128)} %ctf_hbm.1, bf16[72,512]{1,0:T(8,128)(2,1)} %refs_hbm.1), custom_call_target="tpu_custom_call" | custom-call | tf_op jit(solution)/shard_map/pallas_call | solution.py:632
  36.8 2.2 %shard_map.87 = (f32[72,1024]{1,0:T(8,128)}, f32[1,1024]{1,0:T(1,128)}) custom-call(f32[4,8,19,128]{3,2,1,0:T(8,128)} %shard_map.86.landed_hbm), custom_call_target="tpu_custom_call" | custom-call | tf_op jit(solution)/shard_map/pallas_call | solution.py:672

commit v8 on v7

--- a/solution.py
+++ b/solution.py
@@ -439,12 +439,12 @@
             multiply_near(order[turn - 2])
         if turn < z_size:
             from_first(order[turn])
-        if turn >= 2:
-            multiply_far(order[turn - 2])
         if turn == 1:
             shift_chunk(chunks.pop(0))
         if 0 < turn <= z_size:
             from_last(order[turn - 1])
+        if turn >= 2:
+            multiply_far(order[turn - 2])
 
     selected = []
     for block in range(cls_size):

time: 39.6 us -> 39.3 us (level)
  no operation moved by 1% of the time
where the time goes in v8:
time: 39.3 us; the launch traced here: 38.8 us
  Pallas kernels  38.1 us (97%)
  between operations  0.64 us (2%)
    pallas_call x1, Pallas kernels, kernel_shards(): pl.pallas_call(functools.partial(e_step_kernel, dom_size, cls_size), out_...  36 us
    pallas_call x1, Pallas kernels, kernel_shards(): pl.pallas_call(functools.partial(unpack_kernel, slot_count // dom_size),...  2.17 us

profile of v8, /device:TPU:0, one launch (start us, length us, event | category | flops | bytes accessed | tf_op | source)
XLA Modules:
  0.0 38.8 jit_solution(13837268975799098599)
XLA Ops:
  0.6 36.0 %shard_map.86.landed_hbm = f32[4,8,19,128]{3,2,1,0:T(8,128)} custom-call(s32[2,3]{1,0:T(2,128)} %bitcast.7, bf16[128,4096]{1,0:T(8,128)(2,1)} %images_hbm.1, s32[1,128]{1,0:T(1,128)} %bitcast.8, s32[1,128]{1,0:T(1,128)} %bitcast.9, f32[1,2048]{1,0:T(1,128)} %bitcast.6, f32[16,2048]{1,0:T(8,128)} %ctf_hbm.1, bf16[72,512]{1,0:T(8,128)(2,1)} %refs_hbm.1), custom_call_target="tpu_custom_call" | custom-call | tf_op jit(solution)/shard_map/pallas_call | solution.py:632
  36.6 2.2 %shard_map.87 = (f32[72,1024]{1,0:T(8,128)}, f32[1,1024]{1,0:T(1,128)}) custom-call(f32[4,8,19,128]{3,2,1,0:T(8,128)} %shard_map.86.landed_hbm), custom_call_target="tpu_custom_call" | custom-call | tf_op jit(solution)/shard_map/pallas_call | solution.py:672
